TPU v7x, 512 devices: a whole 4x4x16 slice. The times are simulated.
512 devices in a mesh: grp: 32 (over y, x, core), rep: 16 (over z).
Axes of the slice: x: 4, y: 4, z: 16, core: 2. Of those that a mesh axis runs over, the one named last changes fastest.
Arguments:
- amplitudes: float32 [2, 112, 512, 512], P(None, None, ('grp', 'rep')), may hold values from -6 to 6
- ladder_ints: bfloat16 [512, 512, 2, 512], P(('grp', 'rep')), may hold values from -0.09375 to 0.09375
- cycle_ints: float32 [112, 512, 112, 2], P(None, ('grp', 'rep')), may hold values from -0.0234375 to 0.0234375
- virt_sym: int32 [512], replicated, may hold values from 0 to 3
Outputs:
- residual: float32 [112, 2, 2, 512], P('rep', None, None, 'grp')
All inputs are finite; a program needn't handle non-finite values.
Results may differ from a plain program's by a relative error of at most 0.0003.
Values sent between devices are 32-bit elements; how exact they have to be, the bound alone decides.
No kernel may reach another device: no remote copies, remote signals or barrier semaphores. Data moves between devices by JAX's collectives and lax.ppermute only.
A program may use at most 64 MiB of HBM per device.

v0:
```python
import jax
import jax.numpy as jnp
from jax import lax
from jax.sharding import PartitionSpec as P


def shards(amplitudes, ladder_ints, cycle_ints, virt_sym):
    groups = lax.axis_size("grp")
    columns = lax.axis_size("rep")
    local_amps = amplitudes[:, :, 0, :]
    local_ints = ladder_ints[0]
    block_size = local_amps.shape[0]
    occupied = local_amps.shape[1]
    virtuals = local_amps.shape[2]
    slab_size = local_ints.shape[1]
    row_count = occupied // columns
    col_count = virtuals // groups
    group_index = lax.axis_index("grp")
    owner = group_index * columns + lax.axis_index("rep")
    own_sym = lax.dynamic_index_in_dim(virt_sym, owner, 0, keepdims=False)
    slab_sym = virt_sym[:slab_size]
    sym_label = jnp.bitwise_xor(
        jnp.bitwise_xor(own_sym, virt_sym)[:, None, None],
        jnp.bitwise_xor(slab_sym[:, None], virt_sym[None, :])[None],
    )
    widened = local_ints.astype(jnp.float32)
    masked = jnp.where(sym_label == 0, widened, jnp.zeros_like(widened))
    partials = jnp.einsum(
        "irjd,dagb->grjiab",
        local_amps.reshape(block_size, columns, row_count, virtuals),
        masked.reshape(virtuals, slab_size, groups, col_count),
        preferred_element_type=jnp.float32,
        precision=lax.Precision.HIGHEST,
    )
    cycle_all = lax.all_gather(cycle_ints, "grp", axis=1, tiled=True)
    cycle_split = cycle_all.reshape(occupied, groups, columns, row_count, slab_size)
    cycle_term = jnp.einsum(
        "kcrja,ikcb->rjiab",
        cycle_split,
        lax.all_to_all(amplitudes, "grp", split_axis=3, concat_axis=2, tiled=True),
        preferred_element_type=jnp.float32,
        precision=lax.Precision.HIGHEST,
    )
    current = lax.dynamic_index_in_dim(partials, group_index, 0, keepdims=False)
    partials = lax.dynamic_update_index_in_dim(partials, current + cycle_term, group_index, 0)
    flattened = partials.reshape(groups * columns, row_count * block_size * slab_size * col_count)
    owned_flat = lax.psum_scatter(flattened, ("grp", "rep"), scatter_dimension=0, tiled=True)[0]
    return owned_flat.reshape(row_count, block_size, slab_size, col_count)


def solution(mesh):
    return jax.shard_map(
        shards,
        mesh=mesh,
        in_specs=(
            P(None, None, ("grp", "rep"), None),
            P(("grp", "rep"), None, None, None),
            P(None, ("grp", "rep"), None, None),
            P(),
        ),
        out_specs=P("rep", None, None, "grp"),
        check_vma=False,
    )
```

profile of v0, /device:TPU:1, one launch (start us, length us, event | category | flops | bytes accessed | tf_op | source)
XLA Modules:
  0.0 586.7 jit_solution(15268461379823825452)
XLA Ops:
  6.5 0.0 copy-start.2
  6.5 0.0 slice-start
  6.5 0.0 copy-start.1
  6.5 0.0 all-gather.2.cloned.1.call-start
  6.5 1.6 copy.42
  8.2 0.0 all-gather.2.cloned.1.call-update
  8.2 1.9 copy.40
  10.1 10.4 %all-to-all-start = ((f32[2,112,1,512]{1,0,2,3:T(2,128)}), f32[2,112,1,512]{1,0,2,3:T(2,128)S(1)}, u32[]{:S(2)}, u32[]{:S(2)}) async-start(f32[2,112,1,512]{1,0,2,3:T(2,128)} %copy.40), calls=%async_computation | async-start | bytes 1048576 | tf_op jit(solution)/shard_map/all_to_all | solution.py:40
  20.5 0.0 all-reduce.3.cloned.1.call-start
  20.6 1.4 copy.38
  22.0 1.3 dynamic_slice.8
  23.3 0.0 copy-done.1
  23.3 1.4 copy.37
  24.7 0.0 copy-done.2
  24.7 0.7 broadcast_xor_fusion.1
  25.4 0.0 slice-done
  25.4 0.1 broadcast_xor_fusion
  25.5 0.3 convert_select_fusion
  25.8 11.8 %fusion.14 = f32[2,32,16,2,16,7]{4,2,5,3,1,0:T(8,128)S(1)} fusion(f32[512,2,32,16,1,1]{0,3,5,4,2,1:T(8,128)S(1)} %bitcast.50, f32[2,16,7,512,1,1]{3,0,2,1,5,4:T(2,128)S(1)} %bitcast.51), kind=kOutput, calls=%fused_computation.8 | convolution fusion | flops 1409286144 | bytes 3473408 | tf_op jit(solution)/shard_map/irjd,dagb->grjiab/dot_general | solution.py:28
  37.6 0.0 copy-start
  37.6 3.0 copy-done
  40.6 2.9 copy.70
  43.6 0.0 all-to-all-done
  43.6 33.5 %all-gather.2.cloned.1.call-done = f32[112,32,112,2]{2,0,3,1:T(8,128)} async-done(((f32[112,1,112,2]{2,0,3,1:T(8,128)}), f32[112,32,112,2]{2,0,3,1:T(8,128)}) %all-gather.2.cloned.1.call-update) | async-done | bytes 3211280 | tf_op jit(solution)/shard_map/all_gather | solution.py:35
  77.2 5.2 copy.43
  82.4 15.9 %fusion.11 = f32[32,16,7,2,2,16]{1,5,2,3,0,4:T(8,128)} fusion(f32[32,16,7,2,2,16]{1,5,2,3,0,4:T(8,128)} %copy.70, s32[]{:T(128)S(6)} %select_n.21, f32[2,112,32,16,1,1]{1,3,2,4,0,5:T(8,128)S(1)} %bitcast.49, f32[112,32,16,7,2,1]{0,1,4,3,2,5:T(8,128)} %bitcast.47, f32[2,32,16,2,16,7]{4,2,5,3,1,0:T(8,128)} %copy-done), kind=kOutput, calls=%fused_computation.7 | convolution fusion | flops 308288512 | bytes 4587524 | tf_op jit(solution)/shard_map/kcrja,ikcb->rjiab/dot_general | solution.py:37
  98.2 10.3 %copy.46 = f32[32,16,7,2,2,16]{1,0,5,4,3,2:T(8,128)} copy(f32[32,16,7,2,2,16]{1,5,2,3,0,4:T(8,128)} %fusion.11) | data formatting | bytes 1835008 | tf_op jit(solution)/shard_map/jit(dynamic_update_index_in_dim)/dynamic_update_slice | solution.py:45
  108.6 7.6 %reshape.51 = f32[512,448]{0,1:T(8,128)} reshape(f32[32,16,7,2,2,16]{1,0,5,4,3,2:T(8,128)} %copy.46) | data formatting | bytes 1835008 | tf_op jit(solution)/shard_map/reshape | solution.py:46
  116.1 0.0 all-reduce.3.cloned.1.call-update
  116.1 461.9 %all-reduce.3.cloned.1.call-done = f32[512,448]{0,1:T(8,128)} async-done(((f32[512,448]{0,1:T(8,128)}), f32[512,448]{0,1:T(8,128)}) %all-reduce.3.cloned.1.call-update) | async-done | bytes 917520
  578.0 1.2 dynamic-slice_reduce_fusion
  579.2 0.7 reshape_squeeze.7
  (1 shorter events, 0.0 us)
Async XLA Ops:
  6.5 18.2 %copy-start.2 = (s32[512]{0:T(512)S(1)}, s32[512]{0:T(512)}, u32[]{:S(2)}) copy-start(s32[512]{0:T(512)} %param.7) | copy-start | bytes 6148
  6.5 18.8 %slice-start = ((s32[512]{0:T(512)}), s32[2]{0:T(128)S(1)}, s32[]{:S(2)}) async-start(s32[512]{0:T(512)} %param.7), calls=%async_computation.3 | async-start | bytes 1024 | tf_op jit(solution)/shard_map/slice | solution.py:21
  6.5 16.7 %copy-start.1 = (bf16[1,512,2,512]{3,2,1,0:T(2,128)(2,1)S(1)}, bf16[1,512,2,512]{3,2,1,0:T(2,128)(2,1)}, u32[]{:S(2)}) copy-start(bf16[1,512,2,512]{3,2,1,0:T(2,128)(2,1)} %param.5) | copy-start | bytes 3145732
  6.5 70.6 %all-gather.2.cloned.1.call-start = ((), (), s32[]{:S(2)}) async-start(), calls=%async_computation.1 | async-start | bytes 3784704 | tf_op jit(solution)/shard_map/all_gather | solution.py:35
  10.1 33.5 %all-to-all-start = ((f32[2,112,1,512]{1,0,2,3:T(2,128)}), f32[2,112,1,512]{1,0,2,3:T(2,128)S(1)}, u32[]{:S(2)}, u32[]{:S(2)}) async-start(f32[2,112,1,512]{1,0,2,3:T(2,128)} %copy.40), calls=%async_computation | async-start | bytes 1048576 | tf_op jit(solution)/shard_map/all_to_all | solution.py:40
  20.5 557.5 %all-reduce.3.cloned.1.call-start = ((), (), s32[]{:S(2)}) async-start(), calls=%async_computation.2 | async-start | bytes 1835008
  37.6 3.0 copy-start
Sparse Core Ops, SparseCore 0:
  10.5 66.6 all-gather.1
  116.3 461.7 all-reduce.2
where the time goes:
time: 587 us
  waiting for transfers between devices  495 us (84%)
  local copies, waits for them, and re-layouts  38.6 us (7%)
  matrix products  27.7 us (5%)
  between operations  13.5 us (2%)
  starting transfers between devices  10.5 us (2%)
    unnamed x3, waiting for transfers between devices  462 us
    all_gather x1, waiting for transfers between devices, shards(): cycle_all = lax.all_gather(cycle_ints, 'grp', axis=1, tiled=True)  33.5 us
    dot_general x1, matrix products, shards(): jnp.einsum('kcrja,ikcb->rjiab', cycle_split, lax.all_to_all(amplitudes, '...  15.9 us
    unnamed x12, local copies, waits for them, and re-layouts  13.5 us
    dot_general x1, matrix products, shards(): jnp.einsum('irjd,dagb->grjiab', local_amps.reshape(block_size, columns, r...  11.8 us
  transfers between devices with their start and end apart: 3, of which 2 were waited for; matrix products, arithmetic and copies ran while one was open for 4% of the time, Pallas kernels for 0%

commit v1 on v0

v1 whole, which is shorter than its diff:
```python
import functools

import jax
import jax.numpy as jnp
from jax import lax
from jax.experimental import pallas as pl
from jax.experimental.pallas import tpu as pltpu
from jax.sharding import PartitionSpec as P

LANES = 128


def halves(value):
    high = value.astype(jnp.bfloat16)
    low = (value - high.astype(jnp.float32)).astype(jnp.bfloat16)
    return high, low


def dot(left, right):
    return jnp.dot(left, right, preferred_element_type=jnp.float32)


def lane_index(rows):
    return lax.broadcasted_iota(jnp.int32, (rows, LANES), 1)


def partial_kernel(owner_of, amps_ref, ints_ref, cycle_ref, sym_ref, sym_scalars, out_ref, wide_ref):
    tiles = 4
    rows = 224
    occupied = 112
    wide_ref[...] = ints_ref[...].astype(jnp.float32)
    own_sym = sym_scalars[owner_of()]
    chunks = [halves(amps_ref[pl.ds(tile, rows, stride=tiles), :]) for tile in range(tiles)]
    left = jnp.concatenate(
        [
            jnp.concatenate([high for high, _ in chunks], axis=1),
            jnp.concatenate([low for _, low in chunks], axis=1),
        ],
        axis=0,
    )
    pad = LANES - occupied
    turned = []
    for a in range(2):
        block = cycle_ref[pl.ds(a, occupied, stride=2), :]
        block = jnp.concatenate([block, jnp.zeros((pad, occupied), jnp.float32)], axis=0)
        block = jnp.concatenate([block, jnp.zeros((LANES, pad), jnp.float32)], axis=1)
        turned.append(block.T[:occupied])
    cycle_high, cycle_low = halves(jnp.concatenate(turned, axis=0))
    cycle_left = jnp.concatenate([cycle_high, cycle_low, cycle_high], axis=1)
    zero_rows = jnp.zeros((pad, 2 * LANES), jnp.bfloat16)
    sym_columns = jnp.concatenate(
        [jnp.broadcast_to(sym_ref[tile : tile + 1, :], (LANES, LANES)).T for tile in range(tiles)], axis=0
    )
    lanes = lane_index(8)
    for tile in range(tiles):
        label = jnp.bitwise_xor(sym_columns, sym_ref[tile : tile + 1, :])
        masked = []
        for a in range(2):
            block = wide_ref[pl.ds(tile * 2 + a, 512, stride=8), :]
            wanted = jnp.bitwise_xor(own_sym, sym_scalars[a])
            masked.append(jnp.where(label == wanted, block, 0.0).astype(jnp.bfloat16))
        both = dot(left, jnp.concatenate(masked, axis=1))
        ladder = both[:rows] + both[rows:]
        high, low = chunks[tile]
        high = jnp.concatenate([high[:occupied], high[occupied:]], axis=1)
        low = jnp.concatenate([low[:occupied], low[occupied:]], axis=1)
        cycle_right = jnp.concatenate([high, zero_rows, high, zero_rows, low, zero_rows], axis=0)
        cycle = dot(cycle_left, cycle_right)
        firsts, seconds = [], []
        for a in range(2):
            total = ladder[:, a * LANES : (a + 1) * LANES] + jnp.concatenate(
                [cycle[a * occupied : (a + 1) * occupied, i * LANES : (i + 1) * LANES] for i in range(2)], axis=0
            )
            firsts.append(total[:LANES].T)
            rest = jnp.concatenate([total[LANES:], jnp.zeros((2 * LANES - rows, LANES), jnp.float32)], axis=0)
            seconds.append(rest.T)
        for part in range(8):
            g = tile * 8 + part
            at = part * 16
            out_ref[g, 0:16, :] = firsts[0][at : at + 16]
            out_ref[g, 16:32, :] = firsts[1][at : at + 16]
            last = seconds[1][at + 8 : at + 16]
            body = [seconds[0][at : at + 8], seconds[0][at + 8 : at + 16], seconds[1][at : at + 8]]
            for piece in range(3):
                moved = pltpu.roll(last, 96 - 32 * piece, 1)
                out_ref[g, 32 + 8 * piece : 40 + 8 * piece, :] = jnp.where(lanes < 96, body[piece], moved)


def middle_kernel(in_ref, out_ref, turned_ref):
    total = in_ref[0]
    for source in range(1, in_ref.shape[0]):
        total = total + in_ref[source]
    lanes = lane_index(8)
    last = jnp.zeros((8, LANES), jnp.float32)
    for piece in range(3):
        moved = pltpu.roll(total[32 + 8 * piece : 40 + 8 * piece], 32 * piece + 32, 1)
        last = jnp.where((lanes >= 32 * piece) & (lanes < 32 * piece + 32), moved, last)
    fill = jnp.zeros((LANES - 32, LANES), jnp.float32)
    turned_ref[0:LANES, :] = jnp.concatenate([total[:32], fill], axis=0).T
    turned_ref[LANES:, :] = jnp.concatenate([total[32:56], last, fill], axis=0).T
    wide = lane_index(16)
    for i in range(2):
        dest = [jnp.zeros((16, LANES), jnp.float32) for _ in range(2)]
        for jj in range(7):
            rows = turned_ref[pl.ds(i * 112 + jj, 16, stride=7), :]
            for a in range(2):
                moved = pltpu.roll(rows, (jj * 16 - a * 16) % LANES, 1)
                dest[a] = jnp.where((wide >= jj * 16) & (wide < jj * 16 + 16), moved, dest[a])
        for a in range(2):
            out_ref[pl.ds(i * 2 + a, 16, stride=4), :] = dest[a]


def last_kernel(in_ref, out_ref):
    total = in_ref[0]
    for source in range(1, in_ref.shape[0]):
        total = total + in_ref[source]
    for jj in range(7):
        for i in range(2):
            out_ref[jj, i] = total[2 * i : 2 * i + 2, jj * 16 : jj * 16 + 16]


def shards(amplitudes, ladder_ints, cycle_ints, virt_sym):
    amps = amplitudes.reshape(896, LANES)
    ints = ladder_ints.reshape(512, 2, 4, LANES).transpose(0, 2, 1, 3).reshape(4096, LANES)
    cycle = cycle_ints.reshape(112, 112, 2).transpose(0, 2, 1).reshape(224, 112)

    def owner_of():
        return lax.axis_index("grp") * 16 + lax.axis_index("rep")

    vmem = pl.BlockSpec(memory_space=pltpu.VMEM)
    smem = pl.BlockSpec(memory_space=pltpu.SMEM)
    partial = pl.pallas_call(
        functools.partial(partial_kernel, owner_of),
        out_shape=jax.ShapeDtypeStruct((32, 56, LANES), jnp.float32),
        in_specs=[vmem, vmem, vmem, vmem, smem],
        out_specs=vmem,
        scratch_shapes=[pltpu.VMEM((4096, LANES), jnp.float32)],
        compiler_params=pltpu.CompilerParams(vmem_limit_bytes=32 * 1024 * 1024),
        name="partial",
    )(amps, ints, cycle, virt_sym.reshape(4, LANES), virt_sym)
    received = lax.all_to_all(partial, "grp", 0, 0, tiled=True)
    middle = pl.pallas_call(
        middle_kernel,
        out_shape=jax.ShapeDtypeStruct((64, LANES), jnp.float32),
        in_specs=[vmem],
        out_specs=vmem,
        scratch_shapes=[pltpu.VMEM((256, LANES), jnp.float32)],
        name="middle",
    )(received)
    received = lax.all_to_all(middle.reshape(16, 4, LANES), "rep", 0, 0, tiled=True)
    return pl.pallas_call(
        last_kernel,
        out_shape=jax.ShapeDtypeStruct((7, 2, 2, 16), jnp.float32),
        in_specs=[vmem],
        out_specs=vmem,
        name="last",
    )(received)


def solution(mesh):
    return jax.shard_map(
        shards,
        mesh=mesh,
        in_specs=(
            P(None, None, ("grp", "rep"), None),
            P(("grp", "rep"), None, None, None),
            P(None, ("grp", "rep"), None, None),
            P(),
        ),
        out_specs=P("rep", None, None, "grp"),
        check_vma=False,
    )
```

time: 587 us -> 60.5 us (0.10)
  waiting for transfers between devices: 495 us -> 0 us
  blocking collectives: 0 us -> 50.7 us
  local copies, waits for them, and re-layouts: 38.6 us -> 3.82 us
  matrix products: 27.7 us -> 0 us
  between operations: 13.5 us -> 0.01 us
  starting transfers between devices: 10.5 us -> 0 us
    unnamed x3 -> x0, waiting for transfers between devices: 462 us -> none
    all_to_all x0 -> x2, blocking collectives: none -> 50.7 us  [the longest x1 26.1 us: shards(): received = lax.all_to_all(partial, 'grp', 0, 0, tiled=True)]
    all_gather x1 -> x0, waiting for transfers between devices: 33.5 us -> none  [shards(): cycle_all = lax.all_gather(cycle_ints, 'grp', axis=1, tiled=True)]
    dot_general x2 -> x0, matrix products: 27.7 us -> none  [the longest x1 15.9 us: shards(): jnp.einsum('kcrja,ikcb->rjiab', cycle_split, lax.all_to_all(amplitudes, '...]
    all_to_all x1 -> x0, starting transfers between devices: 10.4 us -> none  [shards(): lax.all_to_all(amplitudes, 'grp', split_axis=3, concat_axis=2, tiled=True)]
    dynamic_update_slice x1 -> x0, local copies, waits for them, and re-layouts: 10.3 us -> none  [shards(): lax.dynamic_update_index_in_dim(partials, current + cycle_term, group_ind...]
    unnamed x12 -> x8, local copies, waits for them, and re-layouts: 13.5 us -> 3.82 us
    reshape x1 -> x0, local copies, waits for them, and re-layouts: 7.56 us -> none  [shards(): partials.reshape(groups * columns, row_count * block_size * slab_size * c...]
  transfers between devices with their start and end apart: 3 -> 0, of which waited for: 2 -> 0; matrix products, arithmetic and copies ran while one was open for 4% -> 0% of each run, Pallas kernels for 0% -> 0%
where the time goes in v1:
time: 60.5 us; the launch traced here: 60 us
  blocking collectives  50.7 us (84%)
  Pallas kernels  5.45 us (9%)
  local copies, waits for them, and re-layouts  3.82 us (6%)
    all_to_all x1, blocking collectives, shards(): received = lax.all_to_all(partial, 'grp', 0, 0, tiled=True)  26.1 us
    all_to_all x1, blocking collectives, shards(): lax.all_to_all(middle.reshape(16, 4, LANES), 'rep', 0, 0, tiled=True)  24.7 us
    unnamed x8, local copies, waits for them, and re-layouts  3.82 us
    pallas_call x1, Pallas kernels, shards(): pl.pallas_call(middle_kernel, out_shape=jax.ShapeDtypeStruct((64, LANES),...  2.14 us
    pallas_call x1, Pallas kernels, shards(): pl.pallas_call(functools.partial(partial_kernel, owner_of), out_shape=jax...  1.86 us
    pallas_call x1, Pallas kernels, shards(): pl.pallas_call(last_kernel, out_shape=jax.ShapeDtypeStruct((7, 2, 2, 16),...  1.45 us

profile of v1, /device:TPU:1, one launch (start us, length us, event | category | flops | bytes accessed | tf_op | source)
XLA Modules:
  0.0 60.0 jit_solution(18164010320669315623)
XLA Ops:
  0.0 0.0 copy-start.3
  0.0 0.7 %copy-done.3 = s32[512]{0:T(512)S(1)} copy-done((s32[512]{0:T(512)S(1)}, s32[512]{0:T(512)}, u32[]{:S(2)}) %copy-start.3) | copy-done | bytes 2072
  0.7 0.0 copy-start
  0.7 1.2 %copy-done = bf16[1,512,2,512]{3,2,1,0:T(2,128)(2,1)S(1)} copy-done((bf16[1,512,2,512]{3,2,1,0:T(2,128)(2,1)S(1)}, bf16[1,512,2,512]{3,2,1,0:T(2,128)(2,1)}, u32[]{:S(2)}) %copy-start) | copy-done | bytes 1048600
  1.9 0.0 copy-start.1
  1.9 1.0 %copy-done.1 = f32[2,112,1,512]{3,2,1,0:T(1,128)S(1)} copy-done((f32[2,112,1,512]{3,2,1,0:T(1,128)S(1)}, f32[2,112,1,512]{3,2,1,0:T(1,128)}, u32[]{:S(2)}) %copy-start.1) | copy-done | bytes 458776
  2.9 0.0 copy-start.2
  2.9 0.9 %copy-done.2 = f32[112,1,112,2]{2,3,1,0:T(2,128)S(1)} copy-done((f32[112,1,112,2]{2,3,1,0:T(2,128)S(1)}, f32[112,1,112,2]{2,3,1,0:T(2,128)}, u32[]{:S(2)}) %copy-start.2) | copy-done | bytes 100376
  3.8 1.9 %partial.1 = f32[32,56,128]{2,1,0:T(8,128)S(1)} custom-call(f32[896,128]{1,0:T(8,128)S(1)} %bitcast.14, bf16[4096,128]{1,0:T(8,128)(2,1)S(1)} %bitcast.13, f32[224,112]{1,0:T(8,128)S(1)} %bitcast.15, s32[4,128]{1,0:T(4,128)S(1)} %bitcast.16, s32[512]{0:T(512)S(1)} %copy-done.3), custom_call_target="tpu_custom_call" | custom-call | tf_op jit(solution)/shard_map/partial/pallas_call | solution.py:132
  5.7 26.1 %all_to_all.10.in_ref = f32[32,56,128]{2,1,0:T(8,128)} all-to-all(f32[32,56,128]{2,1,0:T(8,128)S(1)} %partial.1), channel_id=1, replica_groups=mesh['grp'=32,'rep'=16] {'grp'}, dimensions={0} | all-to-all | bytes 1835008 | tf_op jit(solution)/shard_map/all_to_all | solution.py:141
  31.8 2.1 %middle.1 = f32[64,128]{1,0:T(8,128)} custom-call(f32[32,56,128]{2,1,0:T(8,128)} %all_to_all.10.in_ref), custom_call_target="tpu_custom_call" | custom-call | tf_op jit(solution)/shard_map/middle/pallas_call | solution.py:142
  33.9 24.7 %all_to_all.11.in_ref = f32[16,4,128]{2,1,0:T(4,128)} all-to-all(f32[16,4,128]{2,1,0:T(4,128)} %bitcast.17), channel_id=1, replica_groups=mesh['grp'=32,'rep'=16] {'rep'}, dimensions={0} | all-to-all | bytes 65536 | tf_op jit(solution)/shard_map/all_to_all | solution.py:150
  58.6 1.4 %last.1 = f32[7,2,2,16]{3,2,1,0:T(2,128)} custom-call(f32[16,4,128]{2,1,0:T(4,128)} %all_to_all.11.in_ref), custom_call_target="tpu_custom_call" | custom-call | tf_op jit(solution)/shard_map/last/pallas_call | solution.py:151
Async XLA Ops:
  0.0 0.7 %copy-start.3 = (s32[512]{0:T(512)S(1)}, s32[512]{0:T(512)}, u32[]{:S(2)}) copy-start(s32[512]{0:T(512)} %sym_scalars.1) | copy-start | bytes 6148
  0.7 1.2 %copy-start = (bf16[1,512,2,512]{3,2,1,0:T(2,128)(2,1)S(1)}, bf16[1,512,2,512]{3,2,1,0:T(2,128)(2,1)}, u32[]{:S(2)}) copy-start(bf16[1,512,2,512]{3,2,1,0:T(2,128)(2,1)} %param.5) | copy-start | bytes 3145732
  1.9 1.0 %copy-start.1 = (f32[2,112,1,512]{3,2,1,0:T(1,128)S(1)}, f32[2,112,1,512]{3,2,1,0:T(1,128)}, u32[]{:S(2)}) copy-start(f32[2,112,1,512]{3,2,1,0:T(1,128)} %param.4) | copy-start | bytes 1376260
  2.9 0.9 %copy-start.2 = (f32[112,1,112,2]{2,3,1,0:T(2,128)S(1)}, f32[112,1,112,2]{2,3,1,0:T(2,128)}, u32[]{:S(2)}) copy-start(f32[112,1,112,2]{2,3,1,0:T(2,128)} %param.6) | copy-start | bytes 301060

commit v2 on v1

--- a/solution.py
+++ b/solution.py
@@ -24,12 +24,36 @@
     return lax.broadcasted_iota(jnp.int32, (rows, LANES), 1)
 
 
-def partial_kernel(owner_of, amps_ref, ints_ref, cycle_ref, sym_ref, sym_scalars, out_ref, wide_ref):
+def packed(firsts, seconds, at, lanes):
+    pieces = [firsts[a][at + half : at + half + 8] for a in range(2) for half in (0, 8)]
+    body = [seconds[0][at : at + 8], seconds[0][at + 8 : at + 16], seconds[1][at : at + 8]]
+    last = seconds[1][at + 8 : at + 16]
+    for piece in range(3):
+        moved = pltpu.roll(last, 96 - 32 * piece, 1)
+        pieces.append(jnp.where(lanes < 96, body[piece], moved))
+    return pieces
+
+
+def partial_kernel(
+    place_of, amps_hbm, ints_hbm, cycle_hbm, sym_hbm, labels_hbm, keep_ref, send_ref,
+    amps_ref, ints_ref, cycle_ref, sym_ref, sym_scalars, wide_ref, sems,
+):
     tiles = 4
     rows = 224
     occupied = 112
-    wide_ref[...] = ints_ref[...].astype(jnp.float32)
-    own_sym = sym_scalars[owner_of()]
+    parts = 4
+    depth = 4096 // parts
+    pairs = [(labels_hbm, sym_scalars), (sym_hbm, sym_ref), (amps_hbm, amps_ref), (cycle_hbm, cycle_ref)]
+    for part in range(parts):
+        at = pl.ds(part * depth, depth)
+        pairs.append((ints_hbm.at[at], ints_ref.at[at]))
+    copies = [pltpu.make_async_copy(source, target, sems.at[n]) for n, (source, target) in enumerate(pairs)]
+    for copy in copies:
+        copy.start()
+    owner, core = place_of()
+    for copy in copies[:4]:
+        copy.wait()
+    own_sym = sym_scalars[owner]
     chunks = [halves(amps_ref[pl.ds(tile, rows, stride=tiles), :]) for tile in range(tiles)]
     left = jnp.concatenate(
         [
@@ -52,6 +76,10 @@
         [jnp.broadcast_to(sym_ref[tile : tile + 1, :], (LANES, LANES)).T for tile in range(tiles)], axis=0
     )
     lanes = lane_index(8)
+    for part in range(parts):
+        copies[4 + part].wait()
+        at = pl.ds(part * depth, depth)
+        wide_ref[at, :] = ints_ref[at, :].astype(jnp.float32)
     for tile in range(tiles):
         label = jnp.bitwise_xor(sym_columns, sym_ref[tile : tile + 1, :])
         masked = []
@@ -74,16 +102,13 @@
             firsts.append(total[:LANES].T)
             rest = jnp.concatenate([total[LANES:], jnp.zeros((2 * LANES - rows, LANES), jnp.float32)], axis=0)
             seconds.append(rest.T)
-        for part in range(8):
-            g = tile * 8 + part
-            at = part * 16
-            out_ref[g, 0:16, :] = firsts[0][at : at + 16]
-            out_ref[g, 16:32, :] = firsts[1][at : at + 16]
-            last = seconds[1][at + 8 : at + 16]
-            body = [seconds[0][at : at + 8], seconds[0][at + 8 : at + 16], seconds[1][at : at + 8]]
-            for piece in range(3):
-                moved = pltpu.roll(last, 96 - 32 * piece, 1)
-                out_ref[g, 32 + 8 * piece : 40 + 8 * piece, :] = jnp.where(lanes < 96, body[piece], moved)
+        for part in range(4):
+            chip = tile * 4 + part
+            blocks = [packed(firsts, seconds, part * 32 + 16 * side, lanes) for side in range(2)]
+            for at in range(0, 56, 8):
+                zero, one = blocks[0][at // 8], blocks[1][at // 8]
+                keep_ref[chip, at : at + 8, :] = jnp.where(core == 0, zero, one)
+                send_ref[chip, at : at + 8, :] = jnp.where(core == 0, one, zero)
 
 
 def middle_kernel(in_ref, out_ref, turned_ref):
@@ -124,21 +149,34 @@
     ints = ladder_ints.reshape(512, 2, 4, LANES).transpose(0, 2, 1, 3).reshape(4096, LANES)
     cycle = cycle_ints.reshape(112, 112, 2).transpose(0, 2, 1).reshape(224, 112)
 
-    def owner_of():
-        return lax.axis_index("grp") * 16 + lax.axis_index("rep")
-
+    def place_of():
+        group = lax.axis_index("grp")
+        return group * 16 + lax.axis_index("rep"), lax.rem(group, 2)
+
+    hbm = pl.BlockSpec(memory_space=pltpu.HBM)
     vmem = pl.BlockSpec(memory_space=pltpu.VMEM)
-    smem = pl.BlockSpec(memory_space=pltpu.SMEM)
-    partial = pl.pallas_call(
-        functools.partial(partial_kernel, owner_of),
-        out_shape=jax.ShapeDtypeStruct((32, 56, LANES), jnp.float32),
-        in_specs=[vmem, vmem, vmem, vmem, smem],
-        out_specs=vmem,
-        scratch_shapes=[pltpu.VMEM((4096, LANES), jnp.float32)],
+    operands = (amps, ints, cycle, virt_sym.reshape(4, LANES), virt_sym)
+    half = jax.ShapeDtypeStruct((16, 56, LANES), jnp.float32)
+    keep, send = pl.pallas_call(
+        functools.partial(partial_kernel, place_of),
+        out_shape=(half, half),
+        in_specs=[hbm] * 5,
+        out_specs=(vmem, vmem),
+        scratch_shapes=[
+            pltpu.VMEM((896, LANES), jnp.float32),
+            pltpu.VMEM((4096, LANES), jnp.bfloat16),
+            pltpu.VMEM((224, 112), jnp.float32),
+            pltpu.VMEM((4, LANES), jnp.int32),
+            pltpu.SMEM((512,), jnp.int32),
+            pltpu.VMEM((4096, LANES), jnp.float32),
+            pltpu.SemaphoreType.DMA((8,)),
+        ],
         compiler_params=pltpu.CompilerParams(vmem_limit_bytes=32 * 1024 * 1024),
         name="partial",
-    )(amps, ints, cycle, virt_sym.reshape(4, LANES), virt_sym)
-    received = lax.all_to_all(partial, "grp", 0, 0, tiled=True)
+    )(*(pltpu.with_memory_space_constraint(array, pltpu.HBM) for array in operands))
+    other = lax.ppermute(send, "grp", [(g, g ^ 1) for g in range(32)])
+    chips = [[2 * chip + core for chip in range(16)] for core in range(2)]
+    received = lax.all_to_all(keep + other, "grp", 0, 0, tiled=True, axis_index_groups=chips)
     middle = pl.pallas_call(
         middle_kernel,
         out_shape=jax.ShapeDtypeStruct((64, LANES), jnp.float32),

time: 60.5 us -> 55.2 us (0.912)
  the two profiles are of different devices: /device:TPU:1 before, /device:TPU:2 now
where the time goes in v2:
time: 55.2 us; the launch traced here: 54.8 us
  blocking collectives  45 us (82%)
  Pallas kernels  6.01 us (11%)
  starting transfers between devices  1.92 us (3%)
  waiting for transfers between devices  1.78 us (3%)
    all_to_all x1, blocking collectives, shards(): lax.all_to_all(middle.reshape(16, 4, LANES), 'rep', 0, 0, tiled=True)  25.9 us
    all_to_all x1, blocking collectives, shards(): lax.all_to_all(keep + other, 'grp', 0, 0, tiled=True, axis_index_groups=c...  19.1 us
    pallas_call x1, Pallas kernels, shards(): pl.pallas_call(functools.partial(partial_kernel, place_of), out_shape=(ha...  2.62 us
    pallas_call x1, Pallas kernels, shards(): pl.pallas_call(middle_kernel, out_shape=jax.ShapeDtypeStruct((64, LANES),...  1.95 us
    ppermute x1, starting transfers between devices, shards(): other = lax.ppermute(send, 'grp', [(g, g ^ 1) for g in range(32)])  1.92 us
    ppermute x1, waiting for transfers between devices, shards(): other = lax.ppermute(send, 'grp', [(g, g ^ 1) for g in range(32)])  1.78 us
    pallas_call x1, Pallas kernels, shards(): pl.pallas_call(last_kernel, out_shape=jax.ShapeDtypeStruct((7, 2, 2, 16),...  1.45 us
  transfers between devices with their start and end apart: 1, of which 1 were waited for; matrix products, arithmetic and copies ran while one was open for 0% of the time, Pallas kernels for 0%

profile of v2, /device:TPU:2, one launch (start us, length us, event | category | flops | bytes accessed | tf_op | source)
XLA Modules:
  0.0 54.8 jit_solution(17018390136544754326)
XLA Ops:
  0.0 2.6 %partial.1 = (f32[16,56,128]{2,1,0:T(8,128)S(1)}, f32[16,56,128]{2,1,0:T(8,128)S(1)}) custom-call(f32[896,128]{1,0:T(8,128)} %bitcast.14, bf16[4096,128]{1,0:T(8,128)(2,1)} %bitcast.13, f32[224,112]{1,0:T(8,128)} %bitcast.16, s32[4,128]{1,0:T(4,128)} %bitcast.17, s32[512]{0:T(512)} %labels_hbm.1), custom_call_target="tpu_custom_call" | custom-call | tf_op jit(solution)/shard_map/partial/pallas_call | solution.py:160
  2.6 1.9 %collective-permute-start = (f32[16,56,128]{2,1,0:T(8,128)S(1)}, f32[16,56,128]{2,1,0:T(8,128)S(1)}, u32[]{:S(2)}, u32[]{:S(2)}) collective-permute-start(f32[16,56,128]{2,1,0:T(8,128)S(1)} %get-tuple-element.8), channel_id=1, source_target_pairs={{0,16},{16,0},{32,48},{48,32},{64,80},{80,64},{96,112},{112,96},{1... | collective-permute-start | bytes 1376264 | tf_op jit(solution)/shard_map/ppermute | solution.py:177
  4.6 1.8 %collective-permute-done = f32[16,56,128]{2,1,0:T(8,128)S(1)} collective-permute-done((f32[16,56,128]{2,1,0:T(8,128)S(1)}, f32[16,56,128]{2,1,0:T(8,128)S(1)}, u32[]{:S(2)}, u32[]{:S(2)}) %collective-permute-start) | collective-permute-done | bytes 458784 | tf_op jit(solution)/shard_map/ppermute | solution.py:177
  6.3 0.1 add.3
  6.4 19.1 %all_to_all.10.in_ref = f32[16,56,128]{2,1,0:T(8,128)} all-to-all(f32[16,56,128]{2,1,0:T(8,128)S(1)} %add.3), channel_id=1, replica_groups={{0,32,64,96,128,160,192,224,256,288,320,352,384,416,448,480},{16,48,80,..., dimensions={0} | all-to-all | bytes 917504 | tf_op jit(solution)/shard_map/all_to_all | solution.py:179
  25.5 1.9 %middle.1 = f32[64,128]{1,0:T(8,128)} custom-call(f32[16,56,128]{2,1,0:T(8,128)} %all_to_all.10.in_ref), custom_call_target="tpu_custom_call" | custom-call | tf_op jit(solution)/shard_map/middle/pallas_call | solution.py:180
  27.5 25.9 %all_to_all.11.in_ref = f32[16,4,128]{2,1,0:T(4,128)} all-to-all(f32[16,4,128]{2,1,0:T(4,128)} %bitcast.15), channel_id=1, replica_groups=mesh['grp'=32,'rep'=16] {'rep'}, dimensions={0} | all-to-all | bytes 65536 | tf_op jit(solution)/shard_map/all_to_all | solution.py:188
  53.4 1.4 %last.1 = f32[7,2,2,16]{3,2,1,0:T(2,128)} custom-call(f32[16,4,128]{2,1,0:T(4,128)} %all_to_all.11.in_ref), custom_call_target="tpu_custom_call" | custom-call | tf_op jit(solution)/shard_map/last/pallas_call | solution.py:189
Async XLA Ops:
  2.6 3.7 %collective-permute-start = (f32[16,56,128]{2,1,0:T(8,128)S(1)}, f32[16,56,128]{2,1,0:T(8,128)S(1)}, u32[]{:S(2)}, u32[]{:S(2)}) collective-permute-start(f32[16,56,128]{2,1,0:T(8,128)S(1)} %get-tuple-element.8), channel_id=1, source_target_pairs={{0,16},{16,0},{32,48},{48,32},{64,80},{80,64},{96,112},{112,96},{1... | collective-permute-start | bytes 1376264 | tf_op jit(solution)/shard_map/ppermute | solution.py:177

commit v3 on v2

v3 whole, which is shorter than its diff:
```python
import functools

import jax
import jax.numpy as jnp
from jax import lax
from jax.experimental import pallas as pl
from jax.experimental.pallas import tpu as pltpu
from jax.sharding import PartitionSpec as P

LANES = 128


def halves(value):
    high = value.astype(jnp.bfloat16)
    low = (value - high.astype(jnp.float32)).astype(jnp.bfloat16)
    return high, low


def dot(left, right):
    return jnp.dot(left, right, preferred_element_type=jnp.float32)


def partial_kernel(
    place_of, amps_hbm, ints_hbm, cycle_hbm, sym_hbm, labels_hbm, keep_ref, send_ref,
    amps_ref, ints_ref, cycle_ref, sym_ref, sym_scalars, wide_ref, turned_ref, sems,
):
    tiles = 4
    occupied = 112
    columns = 16
    rows = 2 * columns * 8
    parts = 4
    depth = 4096 // parts
    pairs = [
        (labels_hbm, sym_scalars),
        (sym_hbm, sym_ref),
        (amps_hbm, amps_ref.at[pl.ds(0, 2 * occupied * tiles)]),
        (cycle_hbm, cycle_ref.at[pl.ds(0, 2 * occupied)]),
    ]
    for part in range(parts):
        at = pl.ds(part * depth, depth)
        pairs.append((ints_hbm.at[at], ints_ref.at[at]))
    copies = [pltpu.make_async_copy(source, target, sems.at[n]) for n, (source, target) in enumerate(pairs)]
    for copy in copies:
        copy.start()
    owner, core = place_of()
    for copy in copies[:4]:
        copy.wait()
    own_sym = sym_scalars[owner]
    amps_ref[pl.ds(2 * occupied * tiles, 8), :] = jnp.zeros((8, LANES), jnp.float32)
    chunks = []
    for tile in range(tiles):
        groups = [
            amps_ref[pl.ds((i * occupied + z * 7) * tiles + tile, 8, stride=tiles), :]
            for i in range(2)
            for z in range(columns)
        ]
        chunks.append(halves(jnp.concatenate(groups, axis=0)))
    left = jnp.concatenate(
        [
            jnp.concatenate([high for high, _ in chunks], axis=1),
            jnp.concatenate([low for _, low in chunks], axis=1),
        ],
        axis=0,
    )
    eighth = lax.broadcasted_iota(jnp.int32, (8, occupied), 0) == 7
    turned = []
    for a in range(2):
        groups = [
            jnp.where(eighth, 0.0, cycle_ref[pl.ds(z * 14 + a, 8, stride=2), :]) for z in range(columns)
        ]
        block = jnp.concatenate(groups, axis=0)
        block = jnp.concatenate([block, jnp.zeros((LANES, LANES - occupied), jnp.float32)], axis=1)
        turned_ref[a] = block.T
        turned += [turned_ref[a, pl.ds(z * 7, 8), :] for z in range(columns)]
    cycle_high, cycle_low = halves(jnp.concatenate(turned, axis=0))
    cycle_left = jnp.concatenate([cycle_high, cycle_low, cycle_high], axis=1)
    sym_columns = jnp.concatenate(
        [jnp.broadcast_to(sym_ref[tile : tile + 1, :], (LANES, LANES)).T for tile in range(tiles)], axis=0
    )
    for part in range(parts):
        copies[4 + part].wait()
        at = pl.ds(part * depth, depth)
        wide_ref[at, :] = ints_ref[at, :].astype(jnp.float32)
    for tile in range(tiles):
        label = jnp.bitwise_xor(sym_columns, sym_ref[tile : tile + 1, :])
        masked = []
        for a in range(2):
            block = wide_ref[pl.ds(tile * 2 + a, 512, stride=8), :]
            wanted = jnp.bitwise_xor(own_sym, sym_scalars[a])
            masked.append(jnp.where(label == wanted, block, 0.0).astype(jnp.bfloat16))
        both = dot(left, jnp.concatenate(masked, axis=1))
        ladder = both[:rows] + both[rows:]
        high, low = chunks[tile]
        right = jnp.concatenate(
            [
                jnp.concatenate([value[:LANES], value[LANES:]], axis=1)
                for value in (high, high, low)
            ],
            axis=0,
        )
        cycle = dot(cycle_left, right)
        blocks = []
        for half in range(2):
            for a in range(2):
                groups = []
                for z in range(8 * half, 8 * half + 8):
                    for i in range(2):
                        first, second = i * LANES, a * LANES
                        groups.append(
                            ladder[first + 8 * z : first + 8 * z + 8, second : second + LANES]
                            + cycle[second + 8 * z : second + 8 * z + 8, first : first + LANES]
                        )
                blocks.append(jnp.concatenate(groups, axis=0).T)
        for part in range(4):
            chip = tile * 4 + part
            for n, block in enumerate(blocks):
                zero = block[part * 32 : part * 32 + 16]
                one = block[part * 32 + 16 : part * 32 + 32]
                keep_ref[chip, 16 * n : 16 * n + 16, :] = jnp.where(core == 0, zero, one)
                send_ref[chip, 16 * n : 16 * n + 16, :] = jnp.where(core == 0, one, zero)


def shards(amplitudes, ladder_ints, cycle_ints, virt_sym):
    amps = amplitudes.reshape(896, LANES)
    ints = ladder_ints.reshape(512, 2, 4, LANES).transpose(0, 2, 1, 3).reshape(4096, LANES)
    cycle = cycle_ints.reshape(112, 112, 2).transpose(0, 2, 1).reshape(224, 112)

    def place_of():
        group = lax.axis_index("grp")
        return group * 16 + lax.axis_index("rep"), lax.rem(group, 2)

    hbm = pl.BlockSpec(memory_space=pltpu.HBM)
    vmem = pl.BlockSpec(memory_space=pltpu.VMEM)
    operands = (amps, ints, cycle, virt_sym.reshape(4, LANES), virt_sym)
    half = jax.ShapeDtypeStruct((16, 64, LANES), jnp.float32)
    keep, send = pl.pallas_call(
        functools.partial(partial_kernel, place_of),
        out_shape=(half, half),
        in_specs=[hbm] * 5,
        out_specs=(vmem, vmem),
        scratch_shapes=[
            pltpu.VMEM((904, LANES), jnp.float32),
            pltpu.VMEM((4096, LANES), jnp.bfloat16),
            pltpu.VMEM((232, 112), jnp.float32),
            pltpu.VMEM((4, LANES), jnp.int32),
            pltpu.SMEM((512,), jnp.int32),
            pltpu.VMEM((4096, LANES), jnp.float32),
            pltpu.VMEM((2, LANES, LANES), jnp.float32),
            pltpu.SemaphoreType.DMA((8,)),
        ],
        compiler_params=pltpu.CompilerParams(vmem_limit_bytes=32 * 1024 * 1024),
        name="partial",
    )(*(pltpu.with_memory_space_constraint(array, pltpu.HBM) for array in operands))
    other = lax.ppermute(send, "grp", [(g, g ^ 1) for g in range(32)])
    chips = [[2 * chip + core for chip in range(16)] for core in range(2)]
    received = lax.all_to_all(keep + other, "grp", 0, 0, tiled=True, axis_index_groups=chips)
    summed = received.sum(axis=0).reshape(2, 32, LANES).transpose(0, 2, 1).reshape(16, 4, LANES)
    received = lax.all_to_all(summed, "rep", 0, 0, tiled=True)
    return received.sum(axis=0).reshape(2, 8, 2, 16)[:, :7].transpose(1, 0, 2, 3)


def solution(mesh):
    return jax.shard_map(
        shards,
        mesh=mesh,
        in_specs=(
            P(None, None, ("grp", "rep"), None),
            P(("grp", "rep"), None, None, None),
            P(None, ("grp", "rep"), None, None),
            P(),
        ),
        out_specs=P("rep", None, None, "grp"),
        check_vma=False,
    )
```

time: 55.2 us -> 53.1 us (0.962)
  the two profiles are of different devices: /device:TPU:2 before, /device:TPU:1 now
where the time goes in v3:
time: 53.1 us; the launch traced here: 52.2 us
  blocking collectives  38.1 us (72%)
  starting transfers between devices  8.79 us (17%)
  Pallas kernels  2.69 us (5%)
  waiting for transfers between devices  1.51 us (3%)
  local copies, waits for them, and re-layouts  0.9 us (2%)
    all_to_all x1, blocking collectives, shards(): received = lax.all_to_all(summed, 'rep', 0, 0, tiled=True)  24.5 us
    all_to_all x1, blocking collectives, shards(): lax.all_to_all(keep + other, 'grp', 0, 0, tiled=True, axis_index_groups=c...  13.6 us
    ppermute x1, starting transfers between devices, shards(): other = lax.ppermute(send, 'grp', [(g, g ^ 1) for g in range(32)])  8.79 us
    pallas_call x1, Pallas kernels, shards(): pl.pallas_call(functools.partial(partial_kernel, place_of), out_shape=(ha...  2.69 us
    ppermute x1, waiting for transfers between devices, shards(): other = lax.ppermute(send, 'grp', [(g, g ^ 1) for g in range(32)])  1.51 us
  transfers between devices with their start and end apart: 1, of which 1 were waited for; matrix products, arithmetic and copies ran while one was open for 0% of the time, Pallas kernels for 0%

profile of v3, /device:TPU:1, one launch (start us, length us, event | category | flops | bytes accessed | tf_op | source)
XLA Modules:
  0.0 52.2 jit_solution(13726289886035073135)
XLA Ops:
  0.0 2.7 %partial.1 = (f32[16,64,128]{2,1,0:T(8,128)S(1)}, f32[16,64,128]{2,1,0:T(8,128)S(1)}) custom-call(f32[896,128]{1,0:T(8,128)} %bitcast.18, bf16[4096,128]{1,0:T(8,128)(2,1)} %bitcast.17, f32[224,112]{1,0:T(8,128)} %bitcast.20, s32[4,128]{1,0:T(4,128)} %bitcast.21, s32[512]{0:T(512)} %labels_hbm.1), custom_call_target="tpu_custom_call" | custom-call | tf_op jit(solution)/shard_map/partial/pallas_call | solution.py:136
  2.7 8.8 %collective-permute-start = (f32[16,64,128]{2,1,0:T(8,128)S(1)}, f32[16,64,128]{2,1,0:T(8,128)S(1)}, u32[]{:S(2)}, u32[]{:S(2)}) collective-permute-start(f32[16,64,128]{2,1,0:T(8,128)S(1)} %get-tuple-element.8), channel_id=1, source_target_pairs={{0,16},{16,0},{32,48},{48,32},{64,80},{80,64},{96,112},{112,96},{1... | collective-permute-start | bytes 1572872 | tf_op jit(solution)/shard_map/ppermute | solution.py:154
  11.5 1.5 %collective-permute-done = f32[16,64,128]{2,1,0:T(8,128)S(1)} collective-permute-done((f32[16,64,128]{2,1,0:T(8,128)S(1)}, f32[16,64,128]{2,1,0:T(8,128)S(1)}, u32[]{:S(2)}, u32[]{:S(2)}) %collective-permute-start) | collective-permute-done | bytes 524320 | tf_op jit(solution)/shard_map/ppermute | solution.py:154
  13.0 0.1 add.3
  13.1 13.6 %all_to_all.10 = f32[16,64,128]{2,1,0:T(8,128)S(1)} all-to-all(f32[16,64,128]{2,1,0:T(8,128)S(1)} %add.3), channel_id=1, replica_groups={{0,32,64,96,128,160,192,224,256,288,320,352,384,416,448,480},{16,48,80,..., dimensions={0} | all-to-all | bytes 1048576 | tf_op jit(solution)/shard_map/all_to_all | solution.py:156
  26.7 0.1 copy.9
  26.8 0.1 reshape.34
  26.9 24.5 %all_to_all.11 = f32[16,4,128]{2,1,0:T(4,128)S(1)} all-to-all(f32[16,4,128]{2,1,0:T(4,128)S(1)} %reshape.34), channel_id=1, replica_groups=mesh['grp'=32,'rep'=16] {'rep'}, dimensions={0} | all-to-all | bytes 65536 | tf_op jit(solution)/shard_map/all_to_all | solution.py:158
  51.4 0.1 reshape.35
  51.6 0.6 %copy.10 = f32[7,2,2,16]{3,2,1,0:T(2,128)} copy(f32[7,2,2,16]{3,2,0,1:T(2,128)S(1)} %slice_bitcast_fusion) | data formatting | bytes 3584 | tf_op jit(solution)/shard_map/transpose | solution.py:159
  (3 shorter events, 0.1 us)
Async XLA Ops:
  2.7 10.3 %collective-permute-start = (f32[16,64,128]{2,1,0:T(8,128)S(1)}, f32[16,64,128]{2,1,0:T(8,128)S(1)}, u32[]{:S(2)}, u32[]{:S(2)}) collective-permute-start(f32[16,64,128]{2,1,0:T(8,128)S(1)} %get-tuple-element.8), channel_id=1, source_target_pairs={{0,16},{16,0},{32,48},{48,32},{64,80},{80,64},{96,112},{112,96},{1... | collective-permute-start | bytes 1572872 | tf_op jit(solution)/shard_map/ppermute | solution.py:154

commit v4 on v3

--- a/solution.py
+++ b/solution.py
@@ -8,6 +8,8 @@
 from jax.sharding import PartitionSpec as P
 
 LANES = 128
+REP_ORDER = [(z + 8) % 16 for z in range(16)]
+CHIP_ORDER = [(chip + 10) % 16 for chip in range(16)]
 
 
 def halves(value):
@@ -103,7 +105,7 @@
         for half in range(2):
             for a in range(2):
                 groups = []
-                for z in range(8 * half, 8 * half + 8):
+                for z in REP_ORDER[8 * half : 8 * half + 8]:
                     for i in range(2):
                         first, second = i * LANES, a * LANES
                         groups.append(
@@ -112,7 +114,7 @@
                         )
                 blocks.append(jnp.concatenate(groups, axis=0).T)
         for part in range(4):
-            chip = tile * 4 + part
+            chip = CHIP_ORDER.index(tile * 4 + part)
             for n, block in enumerate(blocks):
                 zero = block[part * 32 : part * 32 + 16]
                 one = block[part * 32 + 16 : part * 32 + 32]
@@ -152,10 +154,10 @@
         name="partial",
     )(*(pltpu.with_memory_space_constraint(array, pltpu.HBM) for array in operands))
     other = lax.ppermute(send, "grp", [(g, g ^ 1) for g in range(32)])
-    chips = [[2 * chip + core for chip in range(16)] for core in range(2)]
+    chips = [[2 * chip + core for chip in CHIP_ORDER] for core in range(2)]
     received = lax.all_to_all(keep + other, "grp", 0, 0, tiled=True, axis_index_groups=chips)
     summed = received.sum(axis=0).reshape(2, 32, LANES).transpose(0, 2, 1).reshape(16, 4, LANES)
-    received = lax.all_to_all(summed, "rep", 0, 0, tiled=True)
+    received = lax.all_to_all(summed, "rep", 0, 0, tiled=True, axis_index_groups=[REP_ORDER])
     return received.sum(axis=0).reshape(2, 8, 2, 16)[:, :7].transpose(1, 0, 2, 3)
 
 

time: 53.1 us -> 44.9 us (0.85)
  blocking collectives: 38.1 us -> 30.1 us
    all_to_all x1, blocking collectives: 24.5 us -> 16.8 us  [shards(): lax.all_to_all(summed, 'rep', 0, 0, tiled=True, axis_index_groups=[REP_OR...]
where the time goes in v4:
time: 44.9 us; the launch traced here: 44.2 us
  blocking collectives  30.1 us (67%)
  starting transfers between devices  8.79 us (20%)
  Pallas kernels  2.71 us (6%)
  waiting for transfers between devices  1.51 us (3%)
  local copies, waits for them, and re-layouts  0.9 us (2%)
    all_to_all x1, blocking collectives, shards(): lax.all_to_all(summed, 'rep', 0, 0, tiled=True, axis_index_groups=[REP_OR...  16.8 us
    all_to_all x1, blocking collectives, shards(): lax.all_to_all(keep + other, 'grp', 0, 0, tiled=True, axis_index_groups=c...  13.4 us
    ppermute x1, starting transfers between devices, shards(): other = lax.ppermute(send, 'grp', [(g, g ^ 1) for g in range(32)])  8.79 us
    pallas_call x1, Pallas kernels, shards(): pl.pallas_call(functools.partial(partial_kernel, place_of), out_shape=(ha...  2.71 us
    ppermute x1, waiting for transfers between devices, shards(): other = lax.ppermute(send, 'grp', [(g, g ^ 1) for g in range(32)])  1.51 us
  transfers between devices with their start and end apart: 1, of which 1 were waited for; matrix products, arithmetic and copies ran while one was open for 0% of the time, Pallas kernels for 0%

profile of v4, /device:TPU:1, one launch (start us, length us, event | category | flops | bytes accessed | tf_op | source)
XLA Modules:
  0.0 44.2 jit_solution(10395226371151589144)
XLA Ops:
  0.0 2.7 %partial.1 = (f32[16,64,128]{2,1,0:T(8,128)S(1)}, f32[16,64,128]{2,1,0:T(8,128)S(1)}) custom-call(f32[896,128]{1,0:T(8,128)} %bitcast.18, bf16[4096,128]{1,0:T(8,128)(2,1)} %bitcast.17, f32[224,112]{1,0:T(8,128)} %bitcast.20, s32[4,128]{1,0:T(4,128)} %bitcast.21, s32[512]{0:T(512)} %labels_hbm.1), custom_call_target="tpu_custom_call" | custom-call | tf_op jit(solution)/shard_map/partial/pallas_call | solution.py:138
  2.7 8.8 %collective-permute-start = (f32[16,64,128]{2,1,0:T(8,128)S(1)}, f32[16,64,128]{2,1,0:T(8,128)S(1)}, u32[]{:S(2)}, u32[]{:S(2)}) collective-permute-start(f32[16,64,128]{2,1,0:T(8,128)S(1)} %get-tuple-element.8), channel_id=1, source_target_pairs={{0,16},{16,0},{32,48},{48,32},{64,80},{80,64},{96,112},{112,96},{1... | collective-permute-start | bytes 1572872 | tf_op jit(solution)/shard_map/ppermute | solution.py:156
  11.5 1.5 %collective-permute-done = f32[16,64,128]{2,1,0:T(8,128)S(1)} collective-permute-done((f32[16,64,128]{2,1,0:T(8,128)S(1)}, f32[16,64,128]{2,1,0:T(8,128)S(1)}, u32[]{:S(2)}, u32[]{:S(2)}) %collective-permute-start) | collective-permute-done | bytes 524320 | tf_op jit(solution)/shard_map/ppermute | solution.py:156
  13.0 0.1 add.3
  13.1 13.4 %all_to_all.10 = f32[16,64,128]{2,1,0:T(8,128)S(1)} all-to-all(f32[16,64,128]{2,1,0:T(8,128)S(1)} %add.3), channel_id=1, replica_groups={{320,352,384,416,448,480,0,32,64,96,128,160,192,224,256,288},{336,368,4..., dimensions={0} | all-to-all | bytes 1048576 | tf_op jit(solution)/shard_map/all_to_all | solution.py:158
  26.5 0.1 copy.9
  26.6 0.1 reshape.34
  26.7 16.8 %all_to_all.11 = f32[16,4,128]{2,1,0:T(4,128)S(1)} all-to-all(f32[16,4,128]{2,1,0:T(4,128)S(1)} %reshape.34), channel_id=1, replica_groups={{8,9,10,11,12,13,14,15,0,1,2,3,4,5,6,7},{24,25,26,27,28,29,30,31,16,17,..., dimensions={0} | all-to-all | bytes 65536 | tf_op jit(solution)/shard_map/all_to_all | solution.py:160
  43.5 0.1 reshape.35
  43.6 0.6 %copy.10 = f32[7,2,2,16]{3,2,1,0:T(2,128)} copy(f32[7,2,2,16]{3,2,0,1:T(2,128)S(1)} %slice_bitcast_fusion) | data formatting | bytes 3584 | tf_op jit(solution)/shard_map/transpose | solution.py:161
  (3 shorter events, 0.1 us)
Async XLA Ops:
  2.7 10.3 %collective-permute-start = (f32[16,64,128]{2,1,0:T(8,128)S(1)}, f32[16,64,128]{2,1,0:T(8,128)S(1)}, u32[]{:S(2)}, u32[]{:S(2)}) collective-permute-start(f32[16,64,128]{2,1,0:T(8,128)S(1)} %get-tuple-element.8), channel_id=1, source_target_pairs={{0,16},{16,0},{32,48},{48,32},{64,80},{80,64},{96,112},{112,96},{1... | collective-permute-start | bytes 1572872 | tf_op jit(solution)/shard_map/ppermute | solution.py:156

commit v5 on v4

v5 whole, which is shorter than its diff:
```python
import functools

import jax
import jax.numpy as jnp
from jax import lax
from jax.experimental import pallas as pl
from jax.experimental.pallas import tpu as pltpu
from jax.sharding import PartitionSpec as P

LANES = 128
REP_ORDER = [(z + 8) % 16 for z in range(16)]
CHIP_ORDER = [(chip + 10) % 16 for chip in range(16)]


def halves(value):
    high = value.astype(jnp.bfloat16)
    low = (value - high.astype(jnp.float32)).astype(jnp.bfloat16)
    return high, low


def dot(left, right):
    return jnp.dot(left, right, preferred_element_type=jnp.float32)


def packed(firsts, seconds, at, lanes):
    pieces = [firsts[a][at + half : at + half + 8] for a in range(2) for half in (0, 8)]
    body = [seconds[0][at : at + 8], seconds[0][at + 8 : at + 16], seconds[1][at : at + 8]]
    last = seconds[1][at + 8 : at + 16]
    for piece in range(3):
        moved = pltpu.roll(last, 96 - 32 * piece, 1)
        pieces.append(jnp.where(lanes < 96, body[piece], moved))
    return pieces


def partial_kernel(
    place_of, amps_hbm, ints_hbm, cycle_hbm, sym_hbm, labels_hbm, keep_ref, send_ref,
    amps_ref, ints_ref, cycle_ref, sym_ref, sym_scalars, wide_ref, turned_ref, sems,
):
    tiles = 4
    occupied = 112
    columns = 16
    rows = 2 * occupied
    parts = 4
    depth = 4096 // parts
    pairs = [
        (amps_hbm, amps_ref),
        (cycle_hbm, cycle_ref),
        (labels_hbm, sym_scalars),
        (sym_hbm, sym_ref),
    ]
    for part in range(parts):
        at = pl.ds(part * depth, depth)
        pairs.append((ints_hbm.at[at], ints_ref.at[at]))
    copies = [pltpu.make_async_copy(source, target, sems.at[n]) for n, (source, target) in enumerate(pairs)]
    for copy in copies:
        copy.start()
    owner, core = place_of()
    for copy in copies[:4]:
        copy.wait()
    own_sym = sym_scalars[owner]
    starts = (7 * REP_ORDER[0], 7 * REP_ORDER[8])
    chunks = []
    for tile in range(tiles):
        groups = [
            amps_ref[pl.ds((i * occupied + start + jj) * tiles + tile, 8, stride=7 * tiles), :]
            for jj in range(7)
            for i in range(2)
            for start in starts
        ]
        chunks.append(halves(jnp.concatenate(groups, axis=0)))
    left = jnp.concatenate(
        [
            jnp.concatenate([high for high, _ in chunks], axis=1),
            jnp.concatenate([low for _, low in chunks], axis=1),
        ],
        axis=0,
    )
    pad = LANES - occupied
    turned = []
    for a in range(2):
        groups = [
            cycle_ref[pl.ds((start + jj) * 2 + a, 8, stride=14), :] for jj in range(7) for start in starts
        ]
        block = jnp.concatenate(groups + [jnp.zeros((pad, occupied), jnp.float32)], axis=0)
        block = jnp.concatenate([block, jnp.zeros((LANES, pad), jnp.float32)], axis=1)
        turned_ref[a] = block.T
        turned += [turned_ref[a, pl.ds(start + jj, 8, stride=7), :] for jj in range(7) for start in starts]
    cycle_high, cycle_low = halves(jnp.concatenate(turned, axis=0))
    cycle_left = jnp.concatenate([cycle_high, cycle_low, cycle_high], axis=1)
    zero_rows = jnp.zeros((pad, 2 * LANES), jnp.bfloat16)
    lanes = lax.broadcasted_iota(jnp.int32, (8, LANES), 1)
    sym_columns = jnp.concatenate(
        [jnp.broadcast_to(sym_ref[tile : tile + 1, :], (LANES, LANES)).T for tile in range(tiles)], axis=0
    )
    cycles = []
    for tile in range(tiles):
        high, low = chunks[tile]
        right = []
        for value in (high, high, low):
            sides = [
                jnp.concatenate([value[16 * (2 * jj + i) : 16 * (2 * jj + i) + 16] for jj in range(7)], axis=0)
                for i in range(2)
            ]
            right += [jnp.concatenate(sides, axis=1), zero_rows]
        right = jnp.concatenate(right, axis=0)
        cycles.append(dot(cycle_left, right))
    for part in range(parts):
        copies[4 + part].wait()
        at = pl.ds(part * depth, depth)
        wide_ref[at, :] = ints_ref[at, :].astype(jnp.float32)
    for tile in range(tiles):
        label = jnp.bitwise_xor(sym_columns, sym_ref[tile : tile + 1, :])
        masked = []
        for a in range(2):
            block = wide_ref[pl.ds(tile * 2 + a, 512, stride=8), :]
            wanted = jnp.bitwise_xor(own_sym, sym_scalars[a])
            masked.append(jnp.where(label == wanted, block, 0.0).astype(jnp.bfloat16))
        both = dot(left, jnp.concatenate(masked, axis=1))
        ladder = both[:rows] + both[rows:]
        firsts, seconds = [], []
        for a in range(2):
            groups = [
                cycles[tile][a * occupied + 16 * jj : a * occupied + 16 * jj + 16, i * LANES : (i + 1) * LANES]
                for jj in range(7)
                for i in range(2)
            ]
            total = ladder[:, a * LANES : (a + 1) * LANES] + jnp.concatenate(groups, axis=0)
            firsts.append(total[:LANES].T)
            rest = jnp.concatenate([total[LANES:], jnp.zeros((2 * LANES - rows, LANES), jnp.float32)], axis=0)
            seconds.append(rest.T)
        for part in range(4):
            chip = CHIP_ORDER.index(tile * 4 + part)
            zero, one = (packed(firsts, seconds, part * 32 + 16 * side, lanes) for side in range(2))
            for n in range(7):
                keep_ref[chip, 8 * n : 8 * n + 8, :] = jnp.where(core == 0, zero[n], one[n])
                send_ref[chip, 8 * n : 8 * n + 8, :] = jnp.where(core == 0, one[n], zero[n])


def shards(amplitudes, ladder_ints, cycle_ints, virt_sym):
    amps = amplitudes.reshape(896, LANES)
    ints = ladder_ints.reshape(512, 2, 4, LANES).transpose(0, 2, 1, 3).reshape(4096, LANES)
    cycle = cycle_ints.reshape(112, 112, 2).transpose(0, 2, 1).reshape(224, 112)

    def place_of():
        group = lax.axis_index("grp")
        return group * 16 + lax.axis_index("rep"), lax.rem(group, 2)

    hbm = pl.BlockSpec(memory_space=pltpu.HBM)
    vmem = pl.BlockSpec(memory_space=pltpu.VMEM)
    operands = (amps, ints, cycle, virt_sym.reshape(4, LANES), virt_sym)
    half = jax.ShapeDtypeStruct((16, 56, LANES), jnp.float32)
    keep, send = pl.pallas_call(
        functools.partial(partial_kernel, place_of),
        out_shape=(half, half),
        in_specs=[hbm] * 5,
        out_specs=(vmem, vmem),
        scratch_shapes=[
            pltpu.VMEM((896, LANES), jnp.float32),
            pltpu.VMEM((4096, LANES), jnp.bfloat16),
            pltpu.VMEM((224, 112), jnp.float32),
            pltpu.VMEM((4, LANES), jnp.int32),
            pltpu.SMEM((512,), jnp.int32),
            pltpu.VMEM((4096, LANES), jnp.float32),
            pltpu.VMEM((2, LANES, LANES), jnp.float32),
            pltpu.SemaphoreType.DMA((8,)),
        ],
        compiler_params=pltpu.CompilerParams(vmem_limit_bytes=32 * 1024 * 1024),
        name="partial",
    )(*(pltpu.with_memory_space_constraint(array, pltpu.HBM) for array in operands))
    other = lax.ppermute(send, "grp", [(g, g ^ 1) for g in range(32)])
    chips = [[2 * chip + core for chip in CHIP_ORDER] for core in range(2)]
    received = lax.all_to_all(keep + other, "grp", 0, 0, tiled=True, axis_index_groups=chips)
    summed = received.sum(axis=0).reshape(56, 8, 16).transpose(2, 1, 0)
    summed = jnp.pad(summed, ((0, 0), (0, 0), (0, 8))).reshape(16, 4, LANES)
    received = lax.all_to_all(summed, "rep", 0, 0, tiled=True, axis_index_groups=[REP_ORDER])
    block = received.sum(axis=0).reshape(8, 64)[:, :56]
    last = block[6:, 32:].reshape(2, 3, 8).transpose(1, 0, 2).reshape(6, 8)
    rest = jnp.concatenate([block[:6, 32:], last], axis=1)
    return jnp.concatenate([block[:, :32], rest], axis=0).reshape(7, 2, 2, 16)


def solution(mesh):
    return jax.shard_map(
        shards,
        mesh=mesh,
        in_specs=(
            P(None, None, ("grp", "rep"), None),
            P(("grp", "rep"), None, None, None),
            P(None, ("grp", "rep"), None, None),
            P(),
        ),
        out_specs=P("rep", None, None, "grp"),
        check_vma=False,
    )
```

time: 44.9 us -> 44.4 us (0.989)
  blocking collectives: 30.1 us -> 29.4 us
    all_to_all x1, blocking collectives: 13.4 us -> 12.6 us  [shards(): lax.all_to_all(keep + other, 'grp', 0, 0, tiled=True, axis_index_groups=c...]
    reshape x2 -> x5, local copies, waits for them, and re-layouts: 0.19 us -> 0.94 us  [the longest x1 0.68 us: shards(): return jnp.concatenate([block[:, :32], rest], axis=0).reshape(7, 2, 2, 16)]
    transpose x3 -> x1, local copies, waits for them, and re-layouts: 0.71 us -> 0.01 us  [shards(): last = block[6:, 32:].reshape(2, 3, 8).transpose(1, 0, 2).reshape(6, 8)]
where the time goes in v5:
time: 44.4 us; the launch traced here: 43.8 us
  blocking collectives  29.4 us (66%)
  starting transfers between devices  8.78 us (20%)
  Pallas kernels  2.72 us (6%)
  waiting for transfers between devices  1.42 us (3%)
  local copies, waits for them, and re-layouts  1.22 us (3%)
    all_to_all x1, blocking collectives, shards(): lax.all_to_all(summed, 'rep', 0, 0, tiled=True, axis_index_groups=[REP_OR...  16.8 us
    all_to_all x1, blocking collectives, shards(): lax.all_to_all(keep + other, 'grp', 0, 0, tiled=True, axis_index_groups=c...  12.6 us
    ppermute x1, starting transfers between devices, shards(): other = lax.ppermute(send, 'grp', [(g, g ^ 1) for g in range(32)])  8.78 us
    pallas_call x1, Pallas kernels, shards(): pl.pallas_call(functools.partial(partial_kernel, place_of), out_shape=(ha...  2.72 us
    ppermute x1, waiting for transfers between devices, shards(): other = lax.ppermute(send, 'grp', [(g, g ^ 1) for g in range(32)])  1.42 us
  transfers between devices with their start and end apart: 1, of which 1 were waited for; matrix products, arithmetic and copies ran while one was open for 0% of the time, Pallas kernels for 0%

profile of v5, /device:TPU:1, one launch (start us, length us, event | category | flops | bytes accessed | tf_op | source)
XLA Modules:
  0.0 43.8 jit_solution(4802819084584748105)
XLA Ops:
  0.0 2.7 %partial.1 = (f32[16,56,128]{2,1,0:T(8,128)S(1)}, f32[16,56,128]{2,1,0:T(8,128)S(1)}) custom-call(f32[896,128]{1,0:T(8,128)} %bitcast.18, bf16[4096,128]{1,0:T(8,128)(2,1)} %bitcast.17, f32[224,112]{1,0:T(8,128)} %bitcast.20, s32[4,128]{1,0:T(4,128)} %bitcast.23, s32[512]{0:T(512)} %labels_hbm.1), custom_call_target="tpu_custom_call" | custom-call | tf_op jit(solution)/shard_map/partial/pallas_call | solution.py:152
  2.7 8.8 %collective-permute-start = (f32[16,56,128]{2,1,0:T(8,128)S(1)}, f32[16,56,128]{2,1,0:T(8,128)S(1)}, u32[]{:S(2)}, u32[]{:S(2)}) collective-permute-start(f32[16,56,128]{2,1,0:T(8,128)S(1)} %get-tuple-element.8), channel_id=1, source_target_pairs={{0,16},{16,0},{32,48},{48,32},{64,80},{80,64},{96,112},{112,96},{1... | collective-permute-start | bytes 1376264 | tf_op jit(solution)/shard_map/ppermute | solution.py:170
  11.5 1.4 %collective-permute-done = f32[16,56,128]{2,1,0:T(8,128)S(1)} collective-permute-done((f32[16,56,128]{2,1,0:T(8,128)S(1)}, f32[16,56,128]{2,1,0:T(8,128)S(1)}, u32[]{:S(2)}, u32[]{:S(2)}) %collective-permute-start) | collective-permute-done | bytes 458784 | tf_op jit(solution)/shard_map/ppermute | solution.py:170
  12.9 0.1 add.5
  13.0 12.6 %all_to_all.10 = f32[16,56,128]{2,1,0:T(8,128)S(1)} all-to-all(f32[16,56,128]{2,1,0:T(8,128)S(1)} %add.5), channel_id=1, replica_groups={{320,352,384,416,448,480,0,32,64,96,128,160,192,224,256,288},{336,368,4..., dimensions={0} | all-to-all | bytes 917504 | tf_op jit(solution)/shard_map/all_to_all | solution.py:172
  25.6 0.1 copy.11
  25.8 0.1 reshape.43
  25.9 16.8 %all_to_all.11 = f32[16,4,128]{2,1,0:T(4,128)S(1)} all-to-all(f32[16,4,128]{2,1,0:T(4,128)S(1)} %reshape.43), channel_id=1, replica_groups={{8,9,10,11,12,13,14,15,0,1,2,3,4,5,6,7},{24,25,26,27,28,29,30,31,16,17,..., dimensions={0} | all-to-all | bytes 65536 | tf_op jit(solution)/shard_map/all_to_all | solution.py:175
  42.7 0.1 reshape.44
  42.7 0.1 slice.15
  42.8 0.1 slice.14
  42.9 0.1 reshape.45
  43.0 0.1 maximum_maximum_fusion
  43.1 0.7 %reshape.47 = f32[7,2,2,16]{3,2,1,0:T(2,128)} reshape(f32[14,32]{1,0:T(8,128)S(1)} %maximum_maximum_fusion) | data formatting | bytes 3584 | tf_op jit(solution)/shard_map/reshape | solution.py:179
  (6 shorter events, 0.1 us)
Async XLA Ops:
  2.7 10.2 %collective-permute-start = (f32[16,56,128]{2,1,0:T(8,128)S(1)}, f32[16,56,128]{2,1,0:T(8,128)S(1)}, u32[]{:S(2)}, u32[]{:S(2)}) collective-permute-start(f32[16,56,128]{2,1,0:T(8,128)S(1)} %get-tuple-element.8), channel_id=1, source_target_pairs={{0,16},{16,0},{32,48},{48,32},{64,80},{80,64},{96,112},{112,96},{1... | collective-permute-start | bytes 1376264 | tf_op jit(solution)/shard_map/ppermute | solution.py:170

commit v6 on v5

v6 whole, which is shorter than its diff:
```python
import functools

import jax
import jax.numpy as jnp
from jax import lax
from jax.experimental import pallas as pl
from jax.experimental.pallas import tpu as pltpu
from jax.sharding import PartitionSpec as P

LANES = 128
REP_ORDER = [(z + 8) % 16 for z in range(16)]
CHIP_ORDER = [(chip + 10) % 16 for chip in range(16)]


def halves(value):
    high = value.astype(jnp.bfloat16)
    low = (value - high.astype(jnp.float32)).astype(jnp.bfloat16)
    return high, low


def dot(left, right):
    return jnp.dot(left, right, preferred_element_type=jnp.float32)


def rolled(piece, groups):
    return piece if groups % 8 == 0 else pltpu.roll(piece, 16 * (groups % 8), 1)


def exchanged(pieces, lane_groups):
    turned = [rolled(pieces[s], s) for s in range(8)]
    picked = [turned[-n % 8] for n in range(8)]
    for step in (1, 2, 4):
        take = (lane_groups & step) != 0
        picked = [jnp.where(take, picked[(n - step) % 8], picked[n]) for n in range(8)]
    return [rolled(picked[n], -n) for n in range(8)]


def partial_kernel(
    place_of, amps_hbm, ints_hbm, cycle_hbm, sym_hbm, labels_hbm, keep_ref, send_ref,
    amps_ref, ints_ref, cycle_ref, sym_ref, sym_scalars, wide_ref, turned_ref, sems,
):
    tiles = 4
    occupied = 112
    rows = 2 * occupied
    parts = 2
    depth = 4096 // parts
    pairs = [
        (amps_hbm, amps_ref),
        (cycle_hbm, cycle_ref),
        (labels_hbm, sym_scalars),
        (sym_hbm, sym_ref),
    ]
    for part in range(parts):
        at = pl.ds(part * depth, depth)
        pairs.append((ints_hbm.at[at], ints_ref.at[at]))
    copies = [pltpu.make_async_copy(source, target, sems.at[n]) for n, (source, target) in enumerate(pairs)]
    for copy in copies:
        copy.start()
    owner, core = place_of()
    for copy in copies[:4]:
        copy.wait()
    own_sym = sym_scalars[owner]
    starts = (7 * REP_ORDER[0], 7 * REP_ORDER[8])
    chunks, rights = [], []
    for tile in range(tiles):
        groups = {
            (half, i, jj): amps_ref[pl.ds((i * occupied + start + jj) * tiles + tile, 8, stride=7 * tiles), :]
            for half, start in enumerate(starts)
            for i in range(2)
            for jj in range(7)
        }
        chunks.append(halves(jnp.concatenate(list(groups.values()), axis=0)))
        sides = [
            jnp.concatenate([groups[half, i, jj] for half in range(2) for jj in range(7)], axis=0) for i in range(2)
        ]
        rights.append(halves(jnp.concatenate(sides, axis=1)))
    left = jnp.concatenate(
        [
            jnp.concatenate([high for high, _ in chunks], axis=1),
            jnp.concatenate([low for _, low in chunks], axis=1),
        ],
        axis=0,
    )
    pad = LANES - occupied
    turned = []
    for a in range(2):
        groups = [
            cycle_ref[pl.ds((start + jj) * 2 + a, 8, stride=14), :] for start in starts for jj in range(7)
        ]
        block = jnp.concatenate(groups + [jnp.zeros((pad, occupied), jnp.float32)], axis=0)
        block = jnp.concatenate([block, jnp.zeros((LANES, pad), jnp.float32)], axis=1)
        turned_ref[a] = block.T
        turned += [turned_ref[a, pl.ds(start + jj, 8, stride=7), :] for start in starts for jj in range(7)]
    cycle_high, cycle_low = halves(jnp.concatenate(turned, axis=0))
    cycle_left = jnp.concatenate([cycle_high, cycle_low, cycle_high], axis=1)
    zero_rows = jnp.zeros((pad, 2 * LANES), jnp.bfloat16)
    lane_groups = lax.broadcasted_iota(jnp.int32, (8, LANES), 1) // 16
    sym_columns = jnp.concatenate(
        [jnp.broadcast_to(sym_ref[tile : tile + 1, :], (LANES, LANES)).T for tile in range(tiles)], axis=0
    )
    cycles = []
    for tile in range(tiles):
        high, low = rights[tile]
        right = jnp.concatenate([high, zero_rows, high, zero_rows, low, zero_rows], axis=0)
        cycles.append(dot(cycle_left, right))
    for part in range(parts):
        copies[4 + part].wait()
        at = pl.ds(part * depth, depth)
        wide_ref[at, :] = ints_ref[at, :].astype(jnp.float32)
    for tile in range(tiles):
        label = jnp.bitwise_xor(sym_columns, sym_ref[tile : tile + 1, :])
        masked = []
        for a in range(2):
            block = wide_ref[pl.ds(tile * 2 + a, 512, stride=8), :]
            wanted = jnp.bitwise_xor(own_sym, sym_scalars[a])
            masked.append(jnp.where(label == wanted, block, 0.0).astype(jnp.bfloat16))
        both = dot(left, jnp.concatenate(masked, axis=1))
        ladder = both[:rows] + both[rows:]
        cycle = cycles[tile]
        for jj in range(7):
            pieces = []
            for half in range(2):
                for i in range(2):
                    for a in range(2):
                        row, other = 8 * ((2 * half + i) * 7 + jj), 8 * ((2 * a + half) * 7 + jj)
                        pieces.append(
                            ladder[row : row + 8, a * LANES : (a + 1) * LANES]
                            + cycle[other : other + 8, i * LANES : (i + 1) * LANES]
                        )
            pieces = exchanged(pieces, lane_groups)
            for part in range(4):
                chip = CHIP_ORDER.index(tile * 4 + part)
                zero, one = pieces[2 * part], pieces[2 * part + 1]
                keep_ref[chip, 8 * jj : 8 * jj + 8, :] = jnp.where(core == 0, zero, one)
                send_ref[chip, 8 * jj : 8 * jj + 8, :] = jnp.where(core == 0, one, zero)


def shards(amplitudes, ladder_ints, cycle_ints, virt_sym):
    amps = amplitudes.reshape(896, LANES)
    ints = ladder_ints.reshape(512, 2, 4, LANES).transpose(0, 2, 1, 3).reshape(4096, LANES)
    cycle = cycle_ints.reshape(112, 112, 2).transpose(0, 2, 1).reshape(224, 112)

    def place_of():
        group = lax.axis_index("grp")
        return group * 16 + lax.axis_index("rep"), lax.rem(group, 2)

    hbm = pl.BlockSpec(memory_space=pltpu.HBM)
    vmem = pl.BlockSpec(memory_space=pltpu.VMEM)
    operands = (amps, ints, cycle, virt_sym.reshape(4, LANES), virt_sym)
    half = jax.ShapeDtypeStruct((16, 56, LANES), jnp.float32)
    keep, send = pl.pallas_call(
        functools.partial(partial_kernel, place_of),
        out_shape=(half, half),
        in_specs=[hbm] * 5,
        out_specs=(vmem, vmem),
        scratch_shapes=[
            pltpu.VMEM((896, LANES), jnp.float32),
            pltpu.VMEM((4096, LANES), jnp.bfloat16),
            pltpu.VMEM((224, 112), jnp.float32),
            pltpu.VMEM((4, LANES), jnp.int32),
            pltpu.SMEM((512,), jnp.int32),
            pltpu.VMEM((4096, LANES), jnp.float32),
            pltpu.VMEM((2, LANES, LANES), jnp.float32),
            pltpu.SemaphoreType.DMA((6,)),
        ],
        compiler_params=pltpu.CompilerParams(vmem_limit_bytes=32 * 1024 * 1024),
        name="partial",
    )(*(pltpu.with_memory_space_constraint(array, pltpu.HBM) for array in operands))
    other = lax.ppermute(send, "grp", [(g, g ^ 1) for g in range(32)])
    chips = [[2 * chip + core for chip in CHIP_ORDER] for core in range(2)]
    received = lax.all_to_all(keep + other, "grp", 0, 0, tiled=True, axis_index_groups=chips)
    summed = received.sum(axis=0).reshape(7, 8, 2, 64).transpose(2, 1, 0, 3).reshape(16, 448)
    summed = jnp.pad(summed, ((0, 0), (0, 64))).reshape(16, 4, LANES)
    received = lax.all_to_all(summed, "rep", 0, 0, tiled=True, axis_index_groups=[REP_ORDER])
    return received.sum(axis=0).reshape(512)[:448].reshape(7, 2, 2, 16)


def solution(mesh):
    return jax.shard_map(
        shards,
        mesh=mesh,
        in_specs=(
            P(None, None, ("grp", "rep"), None),
            P(("grp", "rep"), None, None, None),
            P(None, ("grp", "rep"), None, None),
            P(),
        ),
        out_specs=P("rep", None, None, "grp"),
        check_vma=False,
    )
```

time: 44.4 us -> 44.1 us (level)
    reshape x5 -> x3, local copies, waits for them, and re-layouts: 0.94 us -> 0.18 us  [the longest x2 0.17 us: shards(): received.sum(axis=0).reshape(7, 8, 2, 64).transpose(2, 1, 0, 3)]
    slice x2, local copies, waits for them, and re-layouts: 0.15 us -> 0.7 us  [shards(): return received.sum(axis=0).reshape(512)[:448].reshape(7, 2, 2, 16)]
where the time goes in v6:
time: 44.1 us; the launch traced here: 43.4 us
  blocking collectives  29.4 us (67%)
  starting transfers between devices  8.79 us (20%)
  Pallas kernels  2.74 us (6%)
  waiting for transfers between devices  1.42 us (3%)
  local copies, waits for them, and re-layouts  0.91 us (2%)
    all_to_all x1, blocking collectives, shards(): lax.all_to_all(summed, 'rep', 0, 0, tiled=True, axis_index_groups=[REP_OR...  16.8 us
    all_to_all x1, blocking collectives, shards(): lax.all_to_all(keep + other, 'grp', 0, 0, tiled=True, axis_index_groups=c...  12.6 us
    ppermute x1, starting transfers between devices, shards(): other = lax.ppermute(send, 'grp', [(g, g ^ 1) for g in range(32)])  8.79 us
    pallas_call x1, Pallas kernels, shards(): pl.pallas_call(functools.partial(partial_kernel, place_of), out_shape=(ha...  2.74 us
    ppermute x1, waiting for transfers between devices, shards(): other = lax.ppermute(send, 'grp', [(g, g ^ 1) for g in range(32)])  1.42 us
  transfers between devices with their start and end apart: 1, of which 1 were waited for; matrix products, arithmetic and copies ran while one was open for 0% of the time, Pallas kernels for 0%

profile of v6, /device:TPU:1, one launch (start us, length us, event | category | flops | bytes accessed | tf_op | source)
XLA Modules:
  0.0 43.4 jit_solution(14635169098061894775)
XLA Ops:
  0.0 2.7 %partial.1 = (f32[16,56,128]{2,1,0:T(8,128)S(1)}, f32[16,56,128]{2,1,0:T(8,128)S(1)}) custom-call(f32[896,128]{1,0:T(8,128)} %bitcast.14, bf16[4096,128]{1,0:T(8,128)(2,1)} %bitcast.13, f32[224,112]{1,0:T(8,128)} %bitcast.16, s32[4,128]{1,0:T(4,128)} %bitcast.17, s32[512]{0:T(512)} %labels_hbm.1), custom_call_target="tpu_custom_call" | custom-call | tf_op jit(solution)/shard_map/partial/pallas_call | solution.py:151
  2.7 8.8 %collective-permute-start = (f32[16,56,128]{2,1,0:T(8,128)S(1)}, f32[16,56,128]{2,1,0:T(8,128)S(1)}, u32[]{:S(2)}, u32[]{:S(2)}) collective-permute-start(f32[16,56,128]{2,1,0:T(8,128)S(1)} %get-tuple-element.8), channel_id=1, source_target_pairs={{0,16},{16,0},{32,48},{48,32},{64,80},{80,64},{96,112},{112,96},{1... | collective-permute-start | bytes 1376264 | tf_op jit(solution)/shard_map/ppermute | solution.py:169
  11.5 1.4 %collective-permute-done = f32[16,56,128]{2,1,0:T(8,128)S(1)} collective-permute-done((f32[16,56,128]{2,1,0:T(8,128)S(1)}, f32[16,56,128]{2,1,0:T(8,128)S(1)}, u32[]{:S(2)}, u32[]{:S(2)}) %collective-permute-start) | collective-permute-done | bytes 458784 | tf_op jit(solution)/shard_map/ppermute | solution.py:169
  13.0 0.1 add.5
  13.0 12.6 %all_to_all.10 = f32[16,56,128]{2,1,0:T(8,128)S(1)} all-to-all(f32[16,56,128]{2,1,0:T(8,128)S(1)} %add.5), channel_id=1, replica_groups={{320,352,384,416,448,480,0,32,64,96,128,160,192,224,256,288},{336,368,4..., dimensions={0} | all-to-all | bytes 917504 | tf_op jit(solution)/shard_map/all_to_all | solution.py:171
  25.7 0.1 reshape.37
  25.8 0.1 reshape.38
  25.9 16.8 %all_to_all.11 = f32[16,4,128]{2,1,0:T(4,128)S(1)} all-to-all(f32[16,4,128]{2,1,0:T(4,128)S(1)} %reshape.39), channel_id=1, replica_groups={{8,9,10,11,12,13,14,15,0,1,2,3,4,5,6,7},{24,25,26,27,28,29,30,31,16,17,..., dimensions={0} | all-to-all | bytes 65536 | tf_op jit(solution)/shard_map/all_to_all | solution.py:174
  42.7 0.1 slice.6
  42.8 0.6 %slice.8 = f32[7,2,2,16]{3,2,1,0:T(2,128)} slice(f32[8,2,2,16]{3,2,1,0:T(2,128)S(1)} %slice.6), slice={[0:7], [0:2], [0:2], [0:16]} | slice | bytes 3584 | tf_op jit(solution)/shard_map/slice | solution.py:175
  (5 shorter events, 0.1 us)
Async XLA Ops:
  2.7 10.2 %collective-permute-start = (f32[16,56,128]{2,1,0:T(8,128)S(1)}, f32[16,56,128]{2,1,0:T(8,128)S(1)}, u32[]{:S(2)}, u32[]{:S(2)}) collective-permute-start(f32[16,56,128]{2,1,0:T(8,128)S(1)} %get-tuple-element.8), channel_id=1, source_target_pairs={{0,16},{16,0},{32,48},{48,32},{64,80},{80,64},{96,112},{112,96},{1... | collective-permute-start | bytes 1376264 | tf_op jit(solution)/shard_map/ppermute | solution.py:169

commit v7 on v6

v7 whole, which is shorter than its diff:
```python
import functools

import jax
import jax.numpy as jnp
from jax import lax
from jax.experimental import pallas as pl
from jax.experimental.pallas import tpu as pltpu
from jax.sharding import PartitionSpec as P

LANES = 128
REP_ORDER = [(z + 8) % 16 for z in range(16)]
CHIP_ORDER = [(chip + 10) % 16 for chip in range(16)]


def halves(value):
    high = value.astype(jnp.bfloat16)
    low = (value - high.astype(jnp.float32)).astype(jnp.bfloat16)
    return high, low


def dot(left, right):
    return jnp.dot(left, right, preferred_element_type=jnp.float32)


def rolled(piece, groups):
    return piece if groups % 8 == 0 else pltpu.roll(piece, 16 * (groups % 8), 1)


def exchanged(pieces, lane_groups):
    turned = [rolled(pieces[s], s) for s in range(8)]
    picked = [turned[-n % 8] for n in range(8)]
    for step in (1, 2, 4):
        take = (lane_groups & step) != 0
        picked = [jnp.where(take, picked[(n - step) % 8], picked[n]) for n in range(8)]
    return [rolled(picked[n], -n) for n in range(8)]


TILES = 4
OCCUPIED = 112
STARTS = (7 * REP_ORDER[0], 7 * REP_ORDER[8])


def amp_groups(amps_ref, tile):
    return {
        (half, i, jj): amps_ref[pl.ds((i * OCCUPIED + start + jj) * TILES + tile, 8, stride=7 * TILES), :]
        for half, start in enumerate(STARTS)
        for i in range(2)
        for jj in range(7)
    }


def half_blocks(core, kept, left_ref, cycle_left_ref, wide_ref, amps_ref, columns_ref, labels_ref, out_ref):
    lane_groups = lax.broadcasted_iota(jnp.int32, (8, LANES), 1) // 16
    own_parity = (lane_groups & 1) == core
    shift = jnp.where(core == 0, 16, LANES - 16) if kept else jnp.where(core == 0, LANES - 16, 16)

    def merged(same, cross):
        mine = jnp.concatenate([own_parity] * (same.shape[0] // 8), axis=0)
        if kept:
            return jnp.where(mine, same, pltpu.roll(cross, shift, 1))
        return jnp.where(mine, pltpu.roll(same, shift, 1), cross)

    zero_rows = jnp.zeros((LANES - OCCUPIED, 2 * LANES), jnp.bfloat16)
    rows = 2 * OCCUPIED
    for pair in range(2):
        places = (2 * pair + core, 2 * pair + 1 - core)
        groups = [amp_groups(amps_ref, tile) for tile in places]
        sides = []
        for i in range(2):
            order = [(half, i, jj) for half in range(2) for jj in range(7)]
            sides.append(merged(*(jnp.concatenate([group[at] for at in order], axis=0) for group in groups)))
        high, low = halves(jnp.concatenate(sides, axis=1))
        right = jnp.concatenate([high, zero_rows, high, zero_rows, low, zero_rows], axis=0)
        cycle = dot(cycle_left_ref[...], right)
        labels = merged(*(labels_ref[pl.ds(pl.multiple_of(tile * 8, 8), 8), :] for tile in places))
        masked = []
        for a in range(2):
            block = merged(*(wide_ref[pl.ds(tile * 2 + a, 512, stride=8), :] for tile in places))
            wanted = jnp.bitwise_xor(labels, labels_ref[32 + 8 * a : 40 + 8 * a, :])[:1]
            masked.append(jnp.where(columns_ref[...] == wanted, block, 0.0).astype(jnp.bfloat16))
        both = dot(left_ref[...], jnp.concatenate(masked, axis=1))
        ladder = both[:rows] + both[rows:]
        for jj in range(7):
            pieces = []
            for half in range(2):
                for i in range(2):
                    for a in range(2):
                        row, other = 8 * ((2 * half + i) * 7 + jj), 8 * ((2 * a + half) * 7 + jj)
                        pieces.append(
                            ladder[row : row + 8, a * LANES : (a + 1) * LANES]
                            + cycle[other : other + 8, i * LANES : (i + 1) * LANES]
                        )
            for n, piece in enumerate(exchanged(pieces, lane_groups)):
                chip = CHIP_ORDER.index((2 * pair + n % 2) * 4 + n // 2)
                out_ref[chip, 8 * jj : 8 * jj + 8, :] = piece


def send_kernel(
    place_of, amps_hbm, ints_hbm, cycle_hbm, sym_hbm, scalars_hbm,
    send_ref, left_ref, cycle_left_ref, wide_ref, amps_ref, columns_ref, labels_ref,
    ints_ref, cycle_ref, sym_ref, sym_scalars, turned_ref, sems,
):
    parts = 2
    depth = 4096 // parts
    pairs = [
        (amps_hbm, amps_ref),
        (cycle_hbm, cycle_ref),
        (scalars_hbm, sym_scalars),
        (sym_hbm, sym_ref),
    ]
    for part in range(parts):
        at = pl.ds(part * depth, depth)
        pairs.append((ints_hbm.at[at], ints_ref.at[at]))
    copies = [pltpu.make_async_copy(source, target, sems.at[n]) for n, (source, target) in enumerate(pairs)]
    for copy in copies:
        copy.start()
    owner, core = place_of()
    for copy in copies[:4]:
        copy.wait()
    own_sym = sym_scalars[owner]
    for tile in range(TILES):
        row = sym_ref[tile : tile + 1, :]
        labels_ref[8 * tile : 8 * tile + 8, :] = jnp.broadcast_to(row, (8, LANES))
        columns_ref[LANES * tile : LANES * (tile + 1), :] = jnp.broadcast_to(row, (LANES, LANES)).T
    for a in range(2):
        wanted = jnp.bitwise_xor(own_sym, sym_scalars[a])
        labels_ref[32 + 8 * a : 40 + 8 * a, :] = jnp.full((8, LANES), wanted, jnp.int32)
    for tile in range(TILES):
        high, low = halves(jnp.concatenate(list(amp_groups(amps_ref, tile).values()), axis=0))
        left_ref[: 2 * OCCUPIED, LANES * tile : LANES * (tile + 1)] = high
        left_ref[2 * OCCUPIED :, LANES * tile : LANES * (tile + 1)] = low
    pad = LANES - OCCUPIED
    turned = []
    for a in range(2):
        groups = [
            cycle_ref[pl.ds((start + jj) * 2 + a, 8, stride=14), :] for start in STARTS for jj in range(7)
        ]
        block = jnp.concatenate(groups + [jnp.zeros((pad, OCCUPIED), jnp.float32)], axis=0)
        block = jnp.concatenate([block, jnp.zeros((LANES, pad), jnp.float32)], axis=1)
        turned_ref[a] = block.T
        turned += [turned_ref[a, pl.ds(start + jj, 8, stride=7), :] for start in STARTS for jj in range(7)]
    cycle_high, cycle_low = halves(jnp.concatenate(turned, axis=0))
    cycle_left_ref[...] = jnp.concatenate([cycle_high, cycle_low, cycle_high], axis=1)
    for part in range(parts):
        copies[4 + part].wait()
        at = pl.ds(part * depth, depth)
        wide_ref[at, :] = ints_ref[at, :].astype(jnp.float32)
    half_blocks(
        core, False, left_ref, cycle_left_ref, wide_ref, amps_ref, columns_ref, labels_ref, send_ref
    )


def keep_kernel(place_of, left_ref, cycle_left_ref, wide_ref, amps_ref, columns_ref, labels_ref, keep_ref):
    _, core = place_of()
    half_blocks(
        core, True, left_ref, cycle_left_ref, wide_ref, amps_ref, columns_ref, labels_ref, keep_ref
    )


def shards(amplitudes, ladder_ints, cycle_ints, virt_sym):
    amps = amplitudes.reshape(896, LANES)
    ints = ladder_ints.reshape(512, 2, 4, LANES).transpose(0, 2, 1, 3).reshape(4096, LANES)
    cycle = cycle_ints.reshape(112, 112, 2).transpose(0, 2, 1).reshape(224, 112)

    def place_of():
        group = lax.axis_index("grp")
        return group * 16 + lax.axis_index("rep"), lax.rem(group, 2)

    hbm = pl.BlockSpec(memory_space=pltpu.HBM)
    vmem = pl.BlockSpec(memory_space=pltpu.VMEM)
    operands = (amps, ints, cycle, virt_sym.reshape(4, LANES), virt_sym)
    half = jax.ShapeDtypeStruct((16, 56, LANES), jnp.float32)
    send, *rest = pl.pallas_call(
        functools.partial(send_kernel, place_of),
        out_shape=(
            half,
            jax.ShapeDtypeStruct((448, 512), jnp.bfloat16),
            jax.ShapeDtypeStruct((224, 3 * LANES), jnp.bfloat16),
            jax.ShapeDtypeStruct((4096, LANES), jnp.float32),
            jax.ShapeDtypeStruct((896, LANES), jnp.float32),
            jax.ShapeDtypeStruct((512, LANES), jnp.int32),
            jax.ShapeDtypeStruct((48, LANES), jnp.int32),
        ),
        in_specs=[hbm] * 5,
        out_specs=(vmem,) * 7,
        scratch_shapes=[
            pltpu.VMEM((4096, LANES), jnp.bfloat16),
            pltpu.VMEM((224, 112), jnp.float32),
            pltpu.VMEM((4, LANES), jnp.int32),
            pltpu.SMEM((512,), jnp.int32),
            pltpu.VMEM((2, LANES, LANES), jnp.float32),
            pltpu.SemaphoreType.DMA((6,)),
        ],
        compiler_params=pltpu.CompilerParams(vmem_limit_bytes=32 * 1024 * 1024),
        name="send",
    )(*(pltpu.with_memory_space_constraint(array, pltpu.HBM) for array in operands))
    other = lax.ppermute(send, "grp", [(g, g ^ 1) for g in range(32)])
    keep = pl.pallas_call(
        functools.partial(keep_kernel, place_of),
        out_shape=half,
        in_specs=[vmem] * 6,
        out_specs=vmem,
        compiler_params=pltpu.CompilerParams(vmem_limit_bytes=16 * 1024 * 1024),
        cost_estimate=pl.CostEstimate(flops=4 * 10**8, bytes_accessed=3 * 10**6, transcendentals=0),
        name="keep",
    )(*rest)
    chips = [[2 * chip + core for chip in CHIP_ORDER] for core in range(2)]
    received = lax.all_to_all(keep + other, "grp", 0, 0, tiled=True, axis_index_groups=chips)
    summed = received.sum(axis=0).reshape(7, 8, 2, 64).transpose(2, 1, 0, 3).reshape(16, 448)
    summed = jnp.pad(summed, ((0, 0), (0, 64))).reshape(16, 4, LANES)
    received = lax.all_to_all(summed, "rep", 0, 0, tiled=True, axis_index_groups=[REP_ORDER])
    return received.sum(axis=0).reshape(512)[:448].reshape(7, 2, 2, 16)


def solution(mesh):
    return jax.shard_map(
        shards,
        mesh=mesh,
        in_specs=(
            P(None, None, ("grp", "rep"), None),
            P(("grp", "rep"), None, None, None),
            P(None, ("grp", "rep"), None, None),
            P(),
        ),
        out_specs=P("rep", None, None, "grp"),
        check_vma=False,
    )
```

time: 44.1 us -> 44 us (level)
  waiting for transfers between devices: 1.42 us -> 0.43 us
  Pallas kernels: 2.74 us -> 3.63 us
    ppermute x1, waiting for transfers between devices: 1.42 us -> 0.43 us  [shards(): other = lax.ppermute(send, 'grp', [(g, g ^ 1) for g in range(32)])]
    pallas_call x1 -> x2, Pallas kernels: 2.74 us -> 3.63 us  [the longest x1 2.65 us: shards(): pl.pallas_call(functools.partial(send_kernel, place_of), out_shape=(half,...]
  transfers between devices with their start and end apart: 1 -> 1, of which waited for: 1 -> 1; matrix products, arithmetic and copies ran while one was open for 0% -> 0% of each run, Pallas kernels for 0% -> 2%
where the time goes in v7:
time: 44 us; the launch traced here: 43.3 us
  blocking collectives  29.4 us (67%)
  starting transfers between devices  8.8 us (20%)
  Pallas kernels  3.63 us (8%)
  local copies, waits for them, and re-layouts  0.91 us (2%)
    all_to_all x1, blocking collectives, shards(): lax.all_to_all(summed, 'rep', 0, 0, tiled=True, axis_index_groups=[REP_OR...  16.8 us
    all_to_all x1, blocking collectives, shards(): lax.all_to_all(keep + other, 'grp', 0, 0, tiled=True, axis_index_groups=c...  12.6 us
    ppermute x1, starting transfers between devices, shards(): other = lax.ppermute(send, 'grp', [(g, g ^ 1) for g in range(32)])  8.8 us
    pallas_call x1, Pallas kernels, shards(): pl.pallas_call(functools.partial(send_kernel, place_of), out_shape=(half,...  2.65 us
    pallas_call x1, Pallas kernels, shards(): pl.pallas_call(functools.partial(keep_kernel, place_of), out_shape=half,...  0.98 us
  transfers between devices with their start and end apart: 1, of which 1 were waited for; matrix products, arithmetic and copies ran while one was open for 0% of the time, Pallas kernels for 2%

profile of v7, /device:TPU:1, one launch (start us, length us, event | category | flops | bytes accessed | tf_op | source)
XLA Modules:
  0.0 43.3 jit_solution(16030420032657624526)
XLA Ops:
  0.0 2.6 %send.1 = (f32[16,56,128]{2,1,0:T(8,128)S(1)}, bf16[448,512]{1,0:T(8,128)(2,1)S(1)}, bf16[224,384]{1,0:T(8,128)(2,1)S(1)}, f32[4096,128]{1,0:T(8,128)S(1)}, f32[...) custom-call(f32[896,128]{1,0:T(8,128)} %bitcast.14, bf16[4096,128]{1,0:T(8,128)(2,1)} %bitcast.13, ...), custom_call_target="tpu_custom_call" | custom-call | tf_op jit(solution)/shard_map/send/pallas_call | solution.py:173
  2.7 8.8 %collective-permute-start = (f32[16,56,128]{2,1,0:T(8,128)S(1)}, f32[16,56,128]{2,1,0:T(8,128)S(1)}, u32[]{:S(2)}, u32[]{:S(2)}) collective-permute-start(f32[16,56,128]{2,1,0:T(8,128)S(1)} %get-tuple-element.18), channel_id=1, source_target_pairs={{0,16},{16,0},{32,48},{48,32},{64,80},{80,64},{96,112},{112,96},{1... | collective-permute-start | bytes 1376264 | tf_op jit(solution)/shard_map/ppermute | solution.py:197
  11.5 1.0 %keep.1 = f32[16,56,128]{2,1,0:T(8,128)S(1)} custom-call(bf16[448,512]{1,0:T(8,128)(2,1)S(1)} %get-tuple-element.12.left_ref, bf16[224,384]{1,0:T(8,128)(2,1)S(1)} %get-tuple-element.13.cycle_left_ref, f32[4096,128]{1,0:T(8,128)S(1)} %get-tuple-element.14.wide_ref, f32[896,128]{1,0:T(8,128)S(1)} %get-tuple-element.15.amps_ref, ...), custom_call_target="tpu_custom_call" | custom-call | flops 400000000 | bytes 3000000 | tf_op jit(solution)/shard_map/keep/pallas_call | solution.py:198
  12.4 0.4 collective-permute-done
  12.9 0.1 add.5
  12.9 12.6 %all_to_all.10 = f32[16,56,128]{2,1,0:T(8,128)S(1)} all-to-all(f32[16,56,128]{2,1,0:T(8,128)S(1)} %add.5), channel_id=1, replica_groups={{320,352,384,416,448,480,0,32,64,96,128,160,192,224,256,288},{336,368,4..., dimensions={0} | all-to-all | bytes 917504 | tf_op jit(solution)/shard_map/all_to_all | solution.py:208
  25.6 0.1 reshape.37
  25.7 0.1 reshape.38
  25.8 16.8 %all_to_all.11 = f32[16,4,128]{2,1,0:T(4,128)S(1)} all-to-all(f32[16,4,128]{2,1,0:T(4,128)S(1)} %reshape.39), channel_id=1, replica_groups={{8,9,10,11,12,13,14,15,0,1,2,3,4,5,6,7},{24,25,26,27,28,29,30,31,16,17,..., dimensions={0} | all-to-all | bytes 65536 | tf_op jit(solution)/shard_map/all_to_all | solution.py:211
  42.6 0.1 slice.6
  42.7 0.6 %slice.8 = f32[7,2,2,16]{3,2,1,0:T(2,128)} slice(f32[8,2,2,16]{3,2,1,0:T(2,128)S(1)} %slice.6), slice={[0:7], [0:2], [0:2], [0:16]} | slice | bytes 3584 | tf_op jit(solution)/shard_map/slice | solution.py:212
  (5 shorter events, 0.1 us)
Async XLA Ops:
  2.7 10.2 %collective-permute-start = (f32[16,56,128]{2,1,0:T(8,128)S(1)}, f32[16,56,128]{2,1,0:T(8,128)S(1)}, u32[]{:S(2)}, u32[]{:S(2)}) collective-permute-start(f32[16,56,128]{2,1,0:T(8,128)S(1)} %get-tuple-element.18), channel_id=1, source_target_pairs={{0,16},{16,0},{32,48},{48,32},{64,80},{80,64},{96,112},{112,96},{1... | collective-permute-start | bytes 1376264 | tf_op jit(solution)/shard_map/ppermute | solution.py:197

commit v8 on v7

--- a/solution.py
+++ b/solution.py
@@ -100,7 +100,7 @@
     send_ref, left_ref, cycle_left_ref, wide_ref, amps_ref, columns_ref, labels_ref,
     ints_ref, cycle_ref, sym_ref, sym_scalars, turned_ref, sems,
 ):
-    parts = 2
+    parts = 1
     depth = 4096 // parts
     pairs = [
         (amps_hbm, amps_ref),
@@ -189,7 +189,7 @@
             pltpu.VMEM((4, LANES), jnp.int32),
             pltpu.SMEM((512,), jnp.int32),
             pltpu.VMEM((2, LANES, LANES), jnp.float32),
-            pltpu.SemaphoreType.DMA((6,)),
+            pltpu.SemaphoreType.DMA((5,)),
         ],
         compiler_params=pltpu.CompilerParams(vmem_limit_bytes=32 * 1024 * 1024),
         name="send",

time: 44 us -> 44.1 us (level)
  no operation moved by 1% of the time
where the time goes in v8:
time: 44.1 us; the launch traced here: 43.4 us
  blocking collectives  29.4 us (67%)
  starting transfers between devices  8.79 us (20%)
  Pallas kernels  3.69 us (8%)
  local copies, waits for them, and re-layouts  0.91 us (2%)
    all_to_all x1, blocking collectives, shards(): lax.all_to_all(summed, 'rep', 0, 0, tiled=True, axis_index_groups=[REP_OR...  16.8 us
    all_to_all x1, blocking collectives, shards(): lax.all_to_all(keep + other, 'grp', 0, 0, tiled=True, axis_index_groups=c...  12.6 us
    ppermute x1, starting transfers between devices, shards(): other = lax.ppermute(send, 'grp', [(g, g ^ 1) for g in range(32)])  8.79 us
    pallas_call x1, Pallas kernels, shards(): pl.pallas_call(functools.partial(send_kernel, place_of), out_shape=(half,...  2.71 us
    pallas_call x1, Pallas kernels, shards(): pl.pallas_call(functools.partial(keep_kernel, place_of), out_shape=half,...  0.97 us
  transfers between devices with their start and end apart: 1, of which 1 were waited for; matrix products, arithmetic and copies ran while one was open for 0% of the time, Pallas kernels for 2%

profile of v8, /device:TPU:1, one launch (start us, length us, event | category | flops | bytes accessed | tf_op | source)
XLA Modules:
  0.0 43.4 jit_solution(15790990430049553315)
XLA Ops:
  0.0 2.7 %send.1 = (f32[16,56,128]{2,1,0:T(8,128)S(1)}, bf16[448,512]{1,0:T(8,128)(2,1)S(1)}, bf16[224,384]{1,0:T(8,128)(2,1)S(1)}, f32[4096,128]{1,0:T(8,128)S(1)}, f32[...) custom-call(f32[896,128]{1,0:T(8,128)} %bitcast.14, bf16[4096,128]{1,0:T(8,128)(2,1)} %bitcast.13, ...), custom_call_target="tpu_custom_call" | custom-call | tf_op jit(solution)/shard_map/send/pallas_call | solution.py:173
  2.7 8.8 %collective-permute-start = (f32[16,56,128]{2,1,0:T(8,128)S(1)}, f32[16,56,128]{2,1,0:T(8,128)S(1)}, u32[]{:S(2)}, u32[]{:S(2)}) collective-permute-start(f32[16,56,128]{2,1,0:T(8,128)S(1)} %get-tuple-element.18), channel_id=1, source_target_pairs={{0,16},{16,0},{32,48},{48,32},{64,80},{80,64},{96,112},{112,96},{1... | collective-permute-start | bytes 1376264 | tf_op jit(solution)/shard_map/ppermute | solution.py:197
  11.5 1.0 %keep.1 = f32[16,56,128]{2,1,0:T(8,128)S(1)} custom-call(bf16[448,512]{1,0:T(8,128)(2,1)S(1)} %get-tuple-element.12.left_ref, bf16[224,384]{1,0:T(8,128)(2,1)S(1)} %get-tuple-element.13.cycle_left_ref, f32[4096,128]{1,0:T(8,128)S(1)} %get-tuple-element.14.wide_ref, f32[896,128]{1,0:T(8,128)S(1)} %get-tuple-element.15.amps_ref, ...), custom_call_target="tpu_custom_call" | custom-call | flops 400000000 | bytes 3000000 | tf_op jit(solution)/shard_map/keep/pallas_call | solution.py:198
  12.5 0.4 %collective-permute-done = f32[16,56,128]{2,1,0:T(8,128)S(1)} collective-permute-done((f32[16,56,128]{2,1,0:T(8,128)S(1)}, f32[16,56,128]{2,1,0:T(8,128)S(1)}, u32[]{:S(2)}, u32[]{:S(2)}) %collective-permute-start) | collective-permute-done | bytes 458784 | tf_op jit(solution)/shard_map/ppermute | solution.py:197
  12.9 0.1 add.5
  13.0 12.6 %all_to_all.10 = f32[16,56,128]{2,1,0:T(8,128)S(1)} all-to-all(f32[16,56,128]{2,1,0:T(8,128)S(1)} %add.5), channel_id=1, replica_groups={{320,352,384,416,448,480,0,32,64,96,128,160,192,224,256,288},{336,368,4..., dimensions={0} | all-to-all | bytes 917504 | tf_op jit(solution)/shard_map/all_to_all | solution.py:208
  25.6 0.1 reshape.37
  25.8 0.1 reshape.38
  25.9 16.8 %all_to_all.11 = f32[16,4,128]{2,1,0:T(4,128)S(1)} all-to-all(f32[16,4,128]{2,1,0:T(4,128)S(1)} %reshape.39), channel_id=1, replica_groups={{8,9,10,11,12,13,14,15,0,1,2,3,4,5,6,7},{24,25,26,27,28,29,30,31,16,17,..., dimensions={0} | all-to-all | bytes 65536 | tf_op jit(solution)/shard_map/all_to_all | solution.py:211
  42.7 0.1 slice.6
  42.8 0.6 %slice.8 = f32[7,2,2,16]{3,2,1,0:T(2,128)} slice(f32[8,2,2,16]{3,2,1,0:T(2,128)S(1)} %slice.6), slice={[0:7], [0:2], [0:2], [0:16]} | slice | bytes 3584 | tf_op jit(solution)/shard_map/slice | solution.py:212
  (5 shorter events, 0.1 us)
Async XLA Ops:
  2.7 10.2 %collective-permute-start = (f32[16,56,128]{2,1,0:T(8,128)S(1)}, f32[16,56,128]{2,1,0:T(8,128)S(1)}, u32[]{:S(2)}, u32[]{:S(2)}) collective-permute-start(f32[16,56,128]{2,1,0:T(8,128)S(1)} %get-tuple-element.18), channel_id=1, source_target_pairs={{0,16},{16,0},{32,48},{48,32},{64,80},{80,64},{96,112},{112,96},{1... | collective-permute-start | bytes 1376264 | tf_op jit(solution)/shard_map/ppermute | solution.py:197

commit v9 on v7

--- a/solution.py
+++ b/solution.py
@@ -9,7 +9,7 @@
 
 LANES = 128
 REP_ORDER = [(z + 8) % 16 for z in range(16)]
-CHIP_ORDER = [(chip + 10) % 16 for chip in range(16)]
+FIRST_CHIPS = (10, 14)
 
 
 def halves(value):
@@ -60,6 +60,7 @@
             return jnp.where(mine, same, pltpu.roll(cross, shift, 1))
         return jnp.where(mine, pltpu.roll(same, shift, 1), cross)
 
+    first_chip = jnp.where((core == 0) == kept, *FIRST_CHIPS)
     zero_rows = jnp.zeros((LANES - OCCUPIED, 2 * LANES), jnp.bfloat16)
     rows = 2 * OCCUPIED
     for pair in range(2):
@@ -91,7 +92,7 @@
                             + cycle[other : other + 8, i * LANES : (i + 1) * LANES]
                         )
             for n, piece in enumerate(exchanged(pieces, lane_groups)):
-                chip = CHIP_ORDER.index((2 * pair + n % 2) * 4 + n // 2)
+                chip = lax.rem((2 * pair + n % 2) * 4 + n // 2 + 16 - first_chip, 16)
                 out_ref[chip, 8 * jj : 8 * jj + 8, :] = piece
 
 
@@ -204,7 +205,7 @@
         cost_estimate=pl.CostEstimate(flops=4 * 10**8, bytes_accessed=3 * 10**6, transcendentals=0),
         name="keep",
     )(*rest)
-    chips = [[2 * chip + core for chip in CHIP_ORDER] for core in range(2)]
+    chips = [[2 * ((first + n) % 16) + core for n in range(16)] for core, first in enumerate(FIRST_CHIPS)]
     received = lax.all_to_all(keep + other, "grp", 0, 0, tiled=True, axis_index_groups=chips)
     summed = received.sum(axis=0).reshape(7, 8, 2, 64).transpose(2, 1, 0, 3).reshape(16, 448)
     summed = jnp.pad(summed, ((0, 0), (0, 64))).reshape(16, 4, LANES)

time: 44 us -> 44 us (level); the launches traced: 43.3 us -> 43.8 us
  no operation moved by 1% of the time
where the time goes in v9:
time: 44 us; the launch traced here: 43.8 us
  blocking collectives  29.8 us (68%)
  starting transfers between devices  8.79 us (20%)
  Pallas kernels  3.64 us (8%)
  local copies, waits for them, and re-layouts  0.91 us (2%)
    all_to_all x1, blocking collectives, shards(): lax.all_to_all(summed, 'rep', 0, 0, tiled=True, axis_index_groups=[REP_OR...  16.8 us
    all_to_all x1, blocking collectives, shards(): lax.all_to_all(keep + other, 'grp', 0, 0, tiled=True, axis_index_groups=c...  13 us
    ppermute x1, starting transfers between devices, shards(): other = lax.ppermute(send, 'grp', [(g, g ^ 1) for g in range(32)])  8.79 us
    pallas_call x1, Pallas kernels, shards(): pl.pallas_call(functools.partial(send_kernel, place_of), out_shape=(half,...  2.66 us
    pallas_call x1, Pallas kernels, shards(): pl.pallas_call(functools.partial(keep_kernel, place_of), out_shape=half,...  0.99 us
  transfers between devices with their start and end apart: 1, of which 1 were waited for; matrix products, arithmetic and copies ran while one was open for 0% of the time, Pallas kernels for 2%

profile of v9, /device:TPU:1, one launch (start us, length us, event | category | flops | bytes accessed | tf_op | source)
XLA Modules:
  0.0 43.8 jit_solution(12122136966979999169)
XLA Ops:
  0.0 2.7 %send.1 = (f32[16,56,128]{2,1,0:T(8,128)S(1)}, bf16[448,512]{1,0:T(8,128)(2,1)S(1)}, bf16[224,384]{1,0:T(8,128)(2,1)S(1)}, f32[4096,128]{1,0:T(8,128)S(1)}, f32[...) custom-call(f32[896,128]{1,0:T(8,128)} %bitcast.14, bf16[4096,128]{1,0:T(8,128)(2,1)} %bitcast.13, ...), custom_call_target="tpu_custom_call" | custom-call | tf_op jit(solution)/shard_map/send/pallas_call | solution.py:174
  2.7 8.8 %collective-permute-start = (f32[16,56,128]{2,1,0:T(8,128)S(1)}, f32[16,56,128]{2,1,0:T(8,128)S(1)}, u32[]{:S(2)}, u32[]{:S(2)}) collective-permute-start(f32[16,56,128]{2,1,0:T(8,128)S(1)} %get-tuple-element.18), channel_id=1, source_target_pairs={{0,16},{16,0},{32,48},{48,32},{64,80},{80,64},{96,112},{112,96},{1... | collective-permute-start | bytes 1376264 | tf_op jit(solution)/shard_map/ppermute | solution.py:198
  11.5 1.0 %keep.1 = f32[16,56,128]{2,1,0:T(8,128)S(1)} custom-call(bf16[448,512]{1,0:T(8,128)(2,1)S(1)} %get-tuple-element.12.left_ref, bf16[224,384]{1,0:T(8,128)(2,1)S(1)} %get-tuple-element.13.cycle_left_ref, f32[4096,128]{1,0:T(8,128)S(1)} %get-tuple-element.14.wide_ref, f32[896,128]{1,0:T(8,128)S(1)} %get-tuple-element.15.amps_ref, ...), custom_call_target="tpu_custom_call" | custom-call | flops 400000000 | bytes 3000000 | tf_op jit(solution)/shard_map/keep/pallas_call | solution.py:199
  12.5 0.4 collective-permute-done
  12.9 0.1 add.5
  12.9 13.0 %all_to_all.10 = f32[16,56,128]{2,1,0:T(8,128)S(1)} all-to-all(f32[16,56,128]{2,1,0:T(8,128)S(1)} %add.5), channel_id=1, replica_groups={{320,352,384,416,448,480,0,32,64,96,128,160,192,224,256,288},{464,496,1..., dimensions={0} | all-to-all | bytes 917504 | tf_op jit(solution)/shard_map/all_to_all | solution.py:209
  26.0 0.1 reshape.37
  26.1 0.1 reshape.38
  26.2 16.8 %all_to_all.11 = f32[16,4,128]{2,1,0:T(4,128)S(1)} all-to-all(f32[16,4,128]{2,1,0:T(4,128)S(1)} %reshape.39), channel_id=1, replica_groups={{8,9,10,11,12,13,14,15,0,1,2,3,4,5,6,7},{24,25,26,27,28,29,30,31,16,17,..., dimensions={0} | all-to-all | bytes 65536 | tf_op jit(solution)/shard_map/all_to_all | solution.py:212
  43.1 0.1 slice.6
  43.2 0.6 %slice.8 = f32[7,2,2,16]{3,2,1,0:T(2,128)} slice(f32[8,2,2,16]{3,2,1,0:T(2,128)S(1)} %slice.6), slice={[0:7], [0:2], [0:2], [0:16]} | slice | bytes 3584 | tf_op jit(solution)/shard_map/slice | solution.py:213
  (5 shorter events, 0.1 us)
Async XLA Ops:
  2.7 10.2 %collective-permute-start = (f32[16,56,128]{2,1,0:T(8,128)S(1)}, f32[16,56,128]{2,1,0:T(8,128)S(1)}, u32[]{:S(2)}, u32[]{:S(2)}) collective-permute-start(f32[16,56,128]{2,1,0:T(8,128)S(1)} %get-tuple-element.18), channel_id=1, source_target_pairs={{0,16},{16,0},{32,48},{48,32},{64,80},{80,64},{96,112},{112,96},{1... | collective-permute-start | bytes 1376264 | tf_op jit(solution)/shard_map/ppermute | solution.py:198
